TPU v7x, 512 devices: a whole 4x4x16 slice. The times are simulated.
512 devices in a mesh: tok: 4 (over x_lo, core), exp: 128 (over y, x_hi, z).
Axes of the slice: x: 4 (x_hi: 2, x_lo: 2; x = x_hi * 2 + x_lo), y: 4, z: 16, core: 2. Of those that a mesh axis runs over, the one named last changes fastest.
Arguments:
- tokens: bfloat16 [128, 1024, 1024], P('exp', 'tok'), may hold values from -6 to 6
- upstream: bfloat16 [128, 1024, 1024], P('exp', 'tok'), may hold values from -6 to 6
- dispatch: bfloat16 [128, 1024, 128], P('exp', 'tok'), may hold values from 0 to 1, as said below
- combine: bfloat16 [128, 1024, 128], P('exp', 'tok'), may hold values from 0 to 1, as said below
- w_in: bfloat16 [128, 1024, 2048], P('exp', None, 'tok'), may hold values from -0.1875 to 0.1875
- w_out: bfloat16 [128, 2048, 1024], P('exp', 'tok'), may hold values from -0.125 to 0.125
- slot_keys: bfloat16 [1024, 128], replicated, may hold values from -0.1875 to 0.1875
Outputs:
- token_grad: bfloat16 [128, 1024, 1024], P('exp', 'tok')
Inputs may be any that keep to these rules, and one draw needn't show every extreme that they name: `dispatch`: for each image and slot the entries over the image's tokens are positive and sum to one up to rounding. `combine`: for each token the entries over the 128 slots are positive and sum to one up to rounding.
All inputs are finite; a program needn't handle non-finite values.
Results may differ from a plain program's by a relative error of at most 0.025.
Values may be sent and summed in bfloat16 or wider, within the bound.
No kernel may reach another device: no remote copies, remote signals or barrier semaphores. Data moves between devices by JAX's collectives and lax.ppermute only.
A program may use at most 64 MiB of HBM per device.

v0:
```python
import jax
import jax.numpy as jnp
from jax import lax
from jax.sharding import PartitionSpec as P


def in_blocks(value, dim, count):
    lengths = value.shape
    blocks = value.reshape(*lengths[:dim], count, lengths[dim] // count, *lengths[dim + 1 :])
    return jnp.moveaxis(blocks, dim, 0)


def sent_and_summed(value, axis, dim):
    blocks = in_blocks(value, dim, lax.axis_size(axis))
    arrived = lax.all_to_all(blocks, axis, split_axis=0, concat_axis=0, tiled=True)
    return arrived.astype(jnp.float32).sum(axis=0)


def sent_together(arrays, axis, dim, along):
    widths = [a.shape[along] for a in arrays]
    both = jnp.concatenate(arrays, axis=along)
    result = sent_and_summed(both, axis, dim)
    return tuple(jnp.split(result, [sum(widths[:k]) for k in range(1, len(widths))], axis=along))


def in_one_piece(arrays, axis, split_dim, concat_dim, along):
    widths = [a.shape[along] for a in arrays]
    both = jnp.concatenate(arrays, axis=along)
    result = lax.all_to_all(both, axis, split_axis=split_dim, concat_axis=concat_dim, tiled=True)
    return tuple(jnp.split(result, [sum(widths[:k]) for k in range(1, len(widths))], axis=along))


def side_by_side(arrays, axis, dim, along):
    ends, at = ([], 0)
    for a in arrays[:-1]:
        at += a.shape[along]
        ends.append(at)
    both = jnp.concatenate(arrays, axis=along)
    return tuple(jnp.split(lax.all_gather(both, axis, axis=dim, tiled=True), ends, axis=along))


def copy_for_each(value, axis):
    copies = jnp.broadcast_to(value, (lax.axis_size(axis), *value.shape))
    return lax.all_to_all(copies, axis, split_axis=0, concat_axis=0, tiled=True)


def taken_together(value, axis):
    return copy_for_each(value, axis).sum(axis=0)


def gelu_parts(pre_act):
    inside = 0.7978845608 * (pre_act + 0.044715 * pre_act * pre_act * pre_act)
    tanh_val = jnp.tanh(inside)
    gelu_value = 0.5 * pre_act * (1.0 + tanh_val)
    gelu_slope = 0.5 * (1.0 + tanh_val) + 0.5 * pre_act * (
        1.0 - tanh_val * tanh_val
    ) * 0.7978845608 * (1.0 + 3.0 * 0.044715 * pre_act * pre_act)
    return (gelu_value, gelu_slope)


def body(tokens, upstream, dispatch, combine, w_in, w_out, slot_keys):
    slot_input = jnp.einsum("bms,bmd->bsd", dispatch, tokens, preferred_element_type=jnp.float32)
    slot_grad = jnp.einsum("bms,bmd->bsd", combine, upstream, preferred_element_type=jnp.float32)
    summed = sent_together(
        (slot_input.astype(jnp.bfloat16), slot_grad.astype(jnp.bfloat16)), "tok", 2, 0
    )
    sending = (summed[0].astype(jnp.bfloat16), summed[1].astype(jnp.bfloat16))
    arrived = in_one_piece((sending[0], sending[1]), "exp", 1, 0, 2)
    input_rows = arrived[0][:, 0, :]
    grad_rows = arrived[1][:, 0, :]
    input_rows, grad_rows = side_by_side((input_rows, grad_rows), "tok", 1, 0)
    w_first = w_in[0]
    w_second = w_out[0]
    pre_act = jnp.dot(input_rows, w_first, preferred_element_type=jnp.float32)
    gelu_value, gelu_slope = gelu_parts(pre_act)
    hidden = gelu_value.astype(jnp.bfloat16)
    slot_output = jnp.dot(hidden, w_second, preferred_element_type=jnp.float32)
    hidden_grad = jnp.einsum("bd,hd->bh", grad_rows, w_second, preferred_element_type=jnp.float32)
    pre_grad = (hidden_grad * gelu_slope).astype(jnp.bfloat16)
    slot_back = jnp.einsum("bh,dh->bd", pre_grad, w_first, preferred_element_type=jnp.float32)
    partials = sent_together(
        (slot_output.astype(jnp.bfloat16), slot_back.astype(jnp.bfloat16)), "tok", 1, 0
    )
    leaving = (
        partials[0].astype(jnp.bfloat16)[:, None, :],
        partials[1].astype(jnp.bfloat16)[:, None, :],
    )
    returned = in_one_piece((leaving[0], leaving[1]), "exp", 0, 1, 2)
    output_slots, back_slots = returned
    output_slots, back_slots = side_by_side((output_slots, back_slots), "tok", 2, 0)
    comb_grad = jnp.einsum(
        "bmd,bsd->bms", upstream, output_slots, preferred_element_type=jnp.float32
    )
    disp_grad = jnp.einsum("bmd,bsd->bms", tokens, back_slots, preferred_element_type=jnp.float32)
    comb_full = combine.astype(jnp.float32)
    disp_full = dispatch.astype(jnp.float32)
    comb_logit = comb_full * (comb_grad - jnp.sum(comb_full * comb_grad, axis=2, keepdims=True))
    local_totals = jnp.sum(disp_full * disp_grad, axis=1, keepdims=True)
    totals = taken_together(local_totals, "tok")
    disp_logit = disp_full * (disp_grad - totals)
    logit_grad = (comb_logit + disp_logit).astype(jnp.bfloat16)
    result = jnp.einsum("bms,bsd->bmd", dispatch, back_slots, preferred_element_type=jnp.float32)
    result = result + jnp.einsum(
        "bms,ds->bmd", logit_grad, slot_keys, preferred_element_type=jnp.float32
    )
    return result.astype(jnp.bfloat16)


def solution(mesh):
    placed = (
        P("exp", "tok", None),
        P("exp", "tok", None),
        P("exp", "tok", None),
        P("exp", "tok", None),
        P("exp", None, "tok"),
        P("exp", "tok", None),
        P(),
    )
    return jax.shard_map(
        body, mesh=mesh, in_specs=placed, out_specs=P("exp", "tok", None), check_vma=False
    )
```

profile of v0, /device:TPU:1, one launch (start us, length us, event | category | flops | bytes accessed | tf_op | source)
XLA Modules:
  0.0 123.6 jit_solution(2225795978616629511)
XLA Ops:
  0.0 1.4 %convolution_convert_fusion.3 = bf16[128,1024]{1,0:T(8,128)(2,1)S(1)} fusion(bf16[1,256,1024]{2,1,0:T(8,128)(2,1)} %param.7, bf16[1,256,128]{2,1,0:T(8,128)(2,1)} %param.9), kind=kOutput, calls=%fused_computation.7 | convolution fusion | flops 67239936 | bytes 851968 | tf_op jit(solution)/shard_map/bms,bmd->bsd/dot_general | solution.py:62
  1.7 0.8 copy-done.2
  3.0 17.1 %all_to_all.39 = bf16[4,2,128,256]{3,2,1,0:T(8,128)(2,1)S(1)} all-to-all(bf16[4,2,128,256]{3,2,1,0:T(8,128)(2,1)S(1)} %maximum_bitcast_fusion), channel_id=1, replica_groups=mesh['tok'=4,'exp'=128] {'tok'}, dimensions={0} | all-to-all | bytes 1048576 | tf_op jit(solution)/shard_map/all_to_all | solution.py:15
  20.4 0.6 broadcast.44
  21.0 1.4 %reduce.5 = bf16[128,512]{1,0:T(8,128)(2,1)S(1)} reduce(bf16[128,1,512]{2,1,0:T(2,128)(2,1)S(1)} %bitcast.118, bf16[]{:T(256)} %broadcast.44), dimensions={1}, to_apply=%bitcast.115.reduce_sub_computation | reduce | bytes 262146
  22.5 33.6 %all_to_all.40 = bf16[128,2,256]{2,1,0:T(2,128)(2,1)S(1)} all-to-all(bf16[128,2,256]{2,1,0:T(2,128)(2,1)S(1)} %reshape.69), channel_id=1, replica_groups=mesh['tok'=4,'exp'=128] {'exp'}, dimensions={0} | all-to-all | bytes 262144 | tf_op jit(solution)/shard_map/all_to_all | solution.py:29
  56.3 10.0 %all_gather.6 = bf16[256,1024]{1,0:T(8,128)(2,1)S(1)} all-gather(bf16[256,256]{1,0:T(8,128)(2,1)S(1)} %pad_maximum_fusion.2), channel_id=1, replica_groups=mesh['tok'=4,'exp'=128] {'tok'}, dimensions={1}, use_global_device_ids=true | all-gather | bytes 655360 | tf_op jit(solution)/shard_map/all_gather | solution.py:39
  66.6 1.6 %convolution_convert_fusion = bf16[128,1024]{1,0:T(8,128)(2,1)} fusion(bf16[1,512,1024]{2,1,0:T(8,128)(2,1)S(1)} %copy-done, bf16[1,1024,512]{2,1,0:T(8,128)(2,1)S(1)} %copy-done.3, f32[128,512]{1,0:T(8,128)S(1)} %fusion.8, bf16[256,1024]{1,0:T(8,128)(2,1)S(1)} %all_gather.6), kind=kOutput, calls=%fused_computation.4 | convolution fusion | flops 269811712 | bytes 2883584 | tf_op jit(solution)/shard_map/bh,dh->bd/dot_general | solution.py:80
  68.2 0.3 convolution_convert_fusion.1
  68.5 0.6 copy-done.6
  69.2 10.4 %all_to_all.41 = bf16[4,256,256]{2,1,0:T(8,128)(2,1)S(1)} all-to-all(bf16[4,256,256]{2,1,0:T(8,128)(2,1)S(1)} %bitcast.117), channel_id=1, replica_groups=mesh['tok'=4,'exp'=128] {'tok'}, dimensions={0} | all-to-all | bytes 1048576 | tf_op jit(solution)/shard_map/all_to_all | solution.py:15
  79.7 0.7 reduce.6
  80.4 0.7 reshape.71
  81.1 6.2 %all-to-all-start.3 = ((bf16[128,2,256]{2,1,0:T(2,128)(2,1)}), bf16[128,2,256]{2,1,0:T(2,128)(2,1)S(1)}, u32[]{:S(2)}, u32[]{:S(2)}) async-start(bf16[128,2,256]{2,1,0:T(2,128)(2,1)} %reshape.71), calls=%async_computation.3 | async-start | bytes 262144 | tf_op jit(solution)/shard_map/all_to_all | solution.py:29
  87.4 0.7 copy-done.4
  88.2 16.2 %all-to-all-done.3 = bf16[128,2,256]{2,1,0:T(2,128)(2,1)S(1)} async-done(((bf16[128,2,256]{2,1,0:T(2,128)(2,1)}), bf16[128,2,256]{2,1,0:T(2,128)(2,1)S(1)}, u32[]{:S(2)}, u32[]{:S(2)}) %all-to-all-start.3) | async-done | bytes 131104 | tf_op jit(solution)/shard_map/all_to_all | solution.py:29
  104.6 9.9 %all_gather.7 = bf16[2,128,1024]{2,1,0:T(8,128)(2,1)S(1)} all-gather(bf16[2,128,256]{2,1,0:T(8,128)(2,1)S(1)} %pad_maximum_fusion.4), channel_id=1, replica_groups=mesh['tok'=4,'exp'=128] {'tok'}, dimensions={2}, use_global_device_ids=true | all-gather | bytes 655360 | tf_op jit(solution)/shard_map/all_gather | solution.py:39
  114.5 0.4 fusion.36
  114.9 0.6 broadcast_in_dim.13
  115.5 3.4 %all-to-all-start.4 = ((f32[4,1,1,128]{3,2,1,0:T(1,128)}), f32[4,1,1,128]{3,2,1,0:T(1,128)S(1)}, u32[]{:S(2)}, u32[]{:S(2)}) async-start(f32[4,1,1,128]{3,2,1,0:T(1,128)} %broadcast_in_dim.13), calls=%async_computation.4 | async-start | bytes 4096 | tf_op jit(solution)/shard_map/all_to_all | solution.py:44
  118.9 0.3 fusion.33
  119.2 2.7 %all-to-all-done.4 = f32[4,1,1,128]{3,2,1,0:T(1,128)S(1)} async-done(((f32[4,1,1,128]{3,2,1,0:T(1,128)}), f32[4,1,1,128]{3,2,1,0:T(1,128)S(1)}, u32[]{:S(2)}, u32[]{:S(2)}) %all-to-all-start.4) | async-done | bytes 2080 | tf_op jit(solution)/shard_map/all_to_all | solution.py:44
  121.9 0.4 fusion.47
  122.6 1.0 copy.55
  (42 shorter events, 2.4 us)
Async XLA Ops:
  0.0 66.6 %copy-start = (bf16[1,512,1024]{2,1,0:T(8,128)(2,1)S(1)}, bf16[1,512,1024]{2,1,0:T(8,128)(2,1)}, u32[]{:S(2)}) copy-start(bf16[1,512,1024]{2,1,0:T(8,128)(2,1)} %param.12) | copy-start | bytes 3145732
  1.4 1.0 copy-start.2
  1.6 0.9 copy-start.7
  56.1 10.2 %copy-start.3 = (bf16[1,1024,512]{2,1,0:T(8,128)(2,1)S(1)}, bf16[1,1024,512]{2,1,0:T(8,128)(2,1)}, u32[]{:S(2)}) copy-start(bf16[1,1024,512]{2,1,0:T(8,128)(2,1)} %param.11) | copy-start | bytes 3145732
  68.2 0.9 copy-start.6
  81.1 23.3 %all-to-all-start.3 = ((bf16[128,2,256]{2,1,0:T(2,128)(2,1)}), bf16[128,2,256]{2,1,0:T(2,128)(2,1)S(1)}, u32[]{:S(2)}, u32[]{:S(2)}) async-start(bf16[128,2,256]{2,1,0:T(2,128)(2,1)} %reshape.71), calls=%async_computation.3 | async-start | bytes 262144 | tf_op jit(solution)/shard_map/all_to_all | solution.py:29
  87.3 0.8 copy-start.4
  104.6 10.0 %copy-start.1 = (bf16[1,256,1024]{2,1,0:T(8,128)(2,1)S(1)}, bf16[1,256,1024]{2,1,0:T(8,128)(2,1)}, u32[]{:S(2)}) copy-start(bf16[1,256,1024]{2,1,0:T(8,128)(2,1)} %param.7) | copy-start | bytes 1572868
  115.5 6.3 %all-to-all-start.4 = ((f32[4,1,1,128]{3,2,1,0:T(1,128)}), f32[4,1,1,128]{3,2,1,0:T(1,128)S(1)}, u32[]{:S(2)}, u32[]{:S(2)}) async-start(f32[4,1,1,128]{3,2,1,0:T(1,128)} %broadcast_in_dim.13), calls=%async_computation.4 | async-start | bytes 4096 | tf_op jit(solution)/shard_map/all_to_all | solution.py:44
  118.9 3.0 %copy-start.5 = (bf16[1024,128]{1,0:T(8,128)(2,1)S(1)}, bf16[1024,128]{1,0:T(8,128)(2,1)}, u32[]{:S(2)}) copy-start(bf16[1024,128]{1,0:T(8,128)(2,1)} %param.13) | copy-start | bytes 786436
where the time goes:
time: 124 us
  blocking collectives  80.9 us (65%)
  waiting for transfers between devices  18.9 us (15%)
  starting transfers between devices  9.53 us (8%)
  local copies, waits for them, and re-layouts  6.26 us (5%)
  matrix products  5.26 us (4%)
  other arithmetic  2.48 us (2%)
    all_to_all x1, blocking collectives, in_one_piece(): lax.all_to_all(both, axis, split_axis=split_dim, concat_axis=concat_dim,...  33.6 us
    all_to_all x2, blocking collectives, sent_and_summed(): lax.all_to_all(blocks, axis, split_axis=0, concat_axis=0, tiled=True)  27.4 us
    all_gather x2, blocking collectives, side_by_side(): lax.all_gather(both, axis, axis=dim, tiled=True)  19.9 us
    all_to_all x1, waiting for transfers between devices, in_one_piece(): lax.all_to_all(both, axis, split_axis=split_dim, concat_axis=concat_dim,...  16.2 us
    all_to_all x1, starting transfers between devices, in_one_piece(): lax.all_to_all(both, axis, split_axis=split_dim, concat_axis=concat_dim,...  6.17 us
    unnamed x25, local copies, waits for them, and re-layouts  3.96 us
    all_to_all x1, starting transfers between devices, copy_for_each(): return lax.all_to_all(copies, axis, split_axis=0, concat_axis=0, tiled=True)  3.35 us
    all_to_all x1, waiting for transfers between devices, copy_for_each(): return lax.all_to_all(copies, axis, split_axis=0, concat_axis=0, tiled=True)  2.66 us
  transfers between devices with their start and end apart: 2, of which 2 were waited for; matrix products, arithmetic and copies ran while one was open for 0% of the time, Pallas kernels for 0%

commit v1 on v0

v1 whole, which is shorter than its diff:
```python
import jax
import jax.numpy as jnp
from jax import lax
from jax.experimental import pallas as pl
from jax.experimental.pallas import tpu as pltpu
from jax.sharding import Mesh
from jax.sharding import PartitionSpec as P

F32 = jnp.float32
BF16 = jnp.bfloat16
VMEM = pltpu.VMEM
MIB = 1024 * 1024


def dot(a, b, dims):
    return lax.dot_general(a, b, (dims, ((), ())), preferred_element_type=F32)


def slot_sums(disp_hbm, comb_hbm, tok_hbm, up_hbm, out_ref, disp_ref, comb_ref, tok_ref, up_ref, sems):
    quarters, _, both = out_ref.shape
    width = both // 2
    inputs = ((disp_hbm, disp_ref, tok_hbm, tok_ref), (comb_hbm, comb_ref, up_hbm, up_ref))
    copies = []
    for k, (weight_hbm, weight_ref, _, _) in enumerate(inputs):
        copies.append(pltpu.make_async_copy(weight_hbm, weight_ref, sems.at[quarters, k]))
    for q in range(quarters):
        cols = pl.ds(q * width, width)
        for k, (_, _, src, dst) in enumerate(inputs):
            copies.append(pltpu.make_async_copy(src.at[:, cols], dst.at[:, cols], sems.at[q, k]))
    for copy in copies:
        copy.start()
    weights = []
    for k in range(2):
        copies[k].wait()
        weights.append(inputs[k][1][...].T)
    for q in range(quarters):
        for k, (_, _, _, src) in enumerate(inputs):
            copies[2 + 2 * q + k].wait()
            part = dot(weights[k], src[:, q * width : (q + 1) * width], ((1,), (0,)))
            out_ref[q, :, k * width : (k + 1) * width] = part.astype(BF16)


def gelu_parts(pre_act):
    inside = 0.7978845608 * (pre_act + 0.044715 * pre_act * pre_act * pre_act)
    tanh_val = jnp.tanh(inside)
    gelu_value = 0.5 * pre_act * (1.0 + tanh_val)
    gelu_slope = 0.5 * (1.0 + tanh_val) + 0.5 * pre_act * (
        1.0 - tanh_val * tanh_val
    ) * 0.7978845608 * (1.0 + 3.0 * 0.044715 * pre_act * pre_act)
    return gelu_value, gelu_slope


def expert(rows_ref, first_ref, second_ref, out_ref):
    quarters, _, both = rows_ref.shape
    width = both // 2
    pre_act = hidden_grad = 0.0
    for q in range(quarters):
        cols = slice(q * width, (q + 1) * width)
        pre_act += dot(rows_ref[q, :, :width], first_ref[cols, :], ((1,), (0,)))
        hidden_grad += dot(rows_ref[q, :, width:], second_ref[:, cols], ((1,), (1,)))
    value, slope = gelu_parts(pre_act)
    hidden = value.astype(BF16)
    pre_grad = (hidden_grad * slope).astype(BF16)
    for q in range(quarters):
        cols = slice(q * width, (q + 1) * width)
        out_ref[q, :, :width] = dot(hidden, second_ref[:, cols], ((1,), (0,))).astype(BF16)
        out_ref[q, :, width:] = dot(pre_grad, first_ref[cols, :], ((1,), (1,))).astype(BF16)


def with_totals(back_ref, slots_ref, out_ref):
    rows, both = back_ref.shape
    width = both // 2
    out_ref[:rows, :] = back_ref[...]
    product = slots_ref[:, :width].astype(F32) * back_ref[:, width:].astype(F32)
    high = product.astype(BF16)
    low = (product - high.astype(F32)).astype(BF16)
    ones = jnp.ones((16, width), BF16)
    total = dot(ones, high, ((1,), (1,))) + dot(ones, low, ((1,), (1,)))
    total_high = total.astype(BF16)
    out_ref[rows:, :rows] = total_high
    out_ref[rows:, rows : 2 * rows] = (total - total_high.astype(F32)).astype(BF16)
    out_ref[rows:, 2 * rows :] = jnp.zeros((16, both - 2 * rows), BF16)


def tokens_back(rows_ref, tok_ref, up_ref, disp_ref, comb_ref, keys_ref, out_hbm, out_ref, sems):
    quarters, _, both = rows_ref.shape
    slots = disp_ref.shape[1]
    width = both // 2
    comb_grad = disp_grad = totals = 0.0
    for q in range(quarters):
        cols = slice(q * width, (q + 1) * width)
        comb_grad += dot(up_ref[:, cols], rows_ref[q, :slots, :width], ((1,), (1,)))
        disp_grad += dot(tok_ref[:, cols], rows_ref[q, :slots, width:], ((1,), (1,)))
        totals += rows_ref[q, slots:, :slots].astype(F32)
        totals += rows_ref[q, slots:, slots : 2 * slots].astype(F32)
    comb = comb_ref[...].astype(F32)
    disp = disp_ref[...].astype(F32)
    logit = comb * (comb_grad - jnp.sum(comb * comb_grad, axis=1, keepdims=True))
    logit += disp * (disp_grad - totals[:1, :])
    logit = logit.astype(BF16)
    copies = []
    for q in range(quarters):
        cols = slice(q * width, (q + 1) * width)
        part = dot(disp_ref[...], rows_ref[q, :slots, width:], ((1,), (0,)))
        part += dot(logit, keys_ref[cols, :], ((1,), (1,)))
        out_ref[:, cols] = part.astype(BF16)
        block = pl.ds(q * width, width)
        copy = pltpu.make_async_copy(out_ref.at[:, block], out_hbm.at[:, block], sems.at[q])
        copy.start()
        copies.append(copy)
    for copy in copies:
        copy.wait()


def vmem(count):
    return [pl.BlockSpec(memory_space=VMEM)] * count


def hbm(count):
    return [pl.BlockSpec(memory_space=pltpu.HBM)] * count


def params(mib):
    return pltpu.CompilerParams(vmem_limit_bytes=mib * MIB)


def tok_sum(parts, xl, core):
    given = lax.dynamic_index_in_dim(parts, 1 - core, 1, keepdims=False)
    kept = lax.dynamic_index_in_dim(parts, core, 1, keepdims=False)
    arrived = lax.all_gather(given, "core", axis=0)
    arrived = lax.dynamic_index_in_dim(arrived, 1 - core, 0, keepdims=False)

    def half(at):
        return sum(
            lax.dynamic_index_in_dim(v, at, 0, keepdims=False).astype(F32) for v in (kept, arrived)
        )

    across = lax.all_gather(half(1 - xl).astype(BF16), "x_lo", axis=0)
    across = lax.dynamic_index_in_dim(across, 1 - xl, 0, keepdims=False)
    return half(xl) + across.astype(F32)


EXP = ("y", "x_hi", "z")
TOK = ("x_lo", "core")


def exchanged(value):
    rows, cols = value.shape
    blocks = value.reshape(rows, cols // 128, 128)
    return lax.all_to_all(blocks, EXP, split_axis=0, concat_axis=0, tiled=True).reshape(rows, cols)


def body(tokens, upstream, dispatch, combine, w_in, w_out, slot_keys):
    tokens, upstream, dispatch, combine = tokens[0], upstream[0], dispatch[0], combine[0]
    rows, features = tokens.shape
    slots = dispatch.shape[1]
    quarters = 4
    width = features // quarters
    both = 2 * width
    xl, core = lax.axis_index("x_lo"), lax.axis_index("core")
    parts = jax.ShapeDtypeStruct((quarters, slots, both), BF16)

    partial = pl.pallas_call(
        slot_sums,
        out_shape=parts,
        in_specs=hbm(4),
        out_specs=vmem(1)[0],
        scratch_shapes=[
            VMEM((rows, slots), BF16),
            VMEM((rows, slots), BF16),
            VMEM((rows, features), BF16),
            VMEM((rows, features), BF16),
            pltpu.SemaphoreType.DMA((quarters + 1, 2)),
        ],
        compiler_params=params(53),
        name="slot_sums",
    )(dispatch, combine, tokens, upstream)
    summed = tok_sum(partial.reshape(2, 2, slots, both), xl, core).astype(BF16)
    arrived = exchanged(summed)
    images = arrived.shape[0]
    arrived = lax.all_gather(arrived, TOK, axis=0)

    leaving = pl.pallas_call(
        expert,
        out_shape=jax.ShapeDtypeStruct((quarters, images, both), BF16),
        in_specs=vmem(3),
        out_specs=vmem(1)[0],
        compiler_params=params(12),
        name="expert",
    )(arrived, w_in[0], w_out[0])
    leaving = tok_sum(leaving.reshape(2, 2, images, both), xl, core).astype(BF16)
    returned = exchanged(leaving)
    returned = pl.pallas_call(
        with_totals,
        out_shape=jax.ShapeDtypeStruct((slots + 16, both), BF16),
        in_specs=vmem(2),
        out_specs=vmem(1)[0],
        compiler_params=params(4),
        name="with_totals",
    )(returned, summed)
    returned = lax.all_gather(returned, TOK, axis=0)

    result = pl.pallas_call(
        tokens_back,
        out_shape=jax.ShapeDtypeStruct((rows, features), BF16),
        in_specs=vmem(6),
        out_specs=hbm(1)[0],
        scratch_shapes=[VMEM((rows, features), BF16), pltpu.SemaphoreType.DMA((quarters,))],
        compiler_params=params(12),
        name="tokens_back",
    )(returned, tokens, upstream, dispatch, combine, slot_keys)
    return result[None]


def solution(mesh):
    sizes = (2, 2, 4, 2, 16)
    fine = Mesh(mesh.devices.reshape(sizes), TOK + EXP)
    placed = (
        P(EXP, TOK, None),
        P(EXP, TOK, None),
        P(EXP, TOK, None),
        P(EXP, TOK, None),
        P(EXP, None, TOK),
        P(EXP, TOK, None),
        P(),
    )
    return jax.shard_map(
        body, mesh=fine, in_specs=placed, out_specs=P(EXP, TOK, None), check_vma=False
    )
```

time: 124 us -> 107 us (0.86)
  waiting for transfers between devices: 18.9 us -> 0 us
  blocking collectives: 80.9 us -> 99 us
  starting transfers between devices: 9.53 us -> 0 us
  Pallas kernels: 0 us -> 5.59 us
  matrix products: 5.26 us -> 0 us
  local copies, waits for them, and re-layouts: 6.26 us -> 1.92 us
  other arithmetic: 2.48 us -> 0.17 us
    all_gather x2 -> x6, blocking collectives: 19.9 us -> 42.6 us  [the longest x2 11.1 us: tok_sum(): across = lax.all_gather(half(1 - xl).astype(BF16), 'x_lo', axis=0)]
    all_to_all x2 -> x0, waiting for transfers between devices: 18.9 us -> none  [the longest x1 16.2 us: in_one_piece(): lax.all_to_all(both, axis, split_axis=split_dim, concat_axis=concat_dim,...]
    all_to_all x2 -> x0, starting transfers between devices: 9.53 us -> none  [the longest x1 6.17 us: in_one_piece(): lax.all_to_all(both, axis, split_axis=split_dim, concat_axis=concat_dim,...]
    pallas_call x0 -> x4, Pallas kernels: none -> 5.59 us  [the longest x1 2.61 us: body(): pl.pallas_call(slot_sums, out_shape=parts, in_specs=hbm(4), out_specs=vme...]
    dot_general x9 -> x0, matrix products: 5.26 us -> none  [the longest x1 1.58 us: body(): jnp.einsum('bh,dh->bd', pre_grad, w_first, preferred_element_type=jnp.flo...]
    all_to_all x3 -> x2, blocking collectives: 61 us -> 56.4 us  [exchanged(): lax.all_to_all(blocks, EXP, split_axis=0, concat_axis=0, tiled=True)]
    unnamed x25 -> x19, local copies, waits for them, and re-layouts: 3.96 us -> 1.73 us
    unnamed x1 -> x0, other arithmetic: 1.45 us -> none
  transfers between devices with their start and end apart: 2 -> 0, of which waited for: 2 -> 0; matrix products, arithmetic and copies ran while one was open for 0% -> 0% of each run, Pallas kernels for 0% -> 0%
where the time goes in v1:
time: 107 us
  blocking collectives  99 us (93%)
  Pallas kernels  5.59 us (5%)
  local copies, waits for them, and re-layouts  1.92 us (2%)
    all_to_all x2, blocking collectives, exchanged(): lax.all_to_all(blocks, EXP, split_axis=0, concat_axis=0, tiled=True)  56.4 us
    all_gather x2, blocking collectives, tok_sum(): across = lax.all_gather(half(1 - xl).astype(BF16), 'x_lo', axis=0)  11.1 us
    all_gather x2, blocking collectives, tok_sum(): arrived = lax.all_gather(given, 'core', axis=0)  10.9 us
    all_gather x1, blocking collectives, body(): returned = lax.all_gather(returned, TOK, axis=0)  10.6 us
    all_gather x1, blocking collectives, body(): arrived = lax.all_gather(arrived, TOK, axis=0)  9.93 us
    pallas_call x1, Pallas kernels, body(): pl.pallas_call(slot_sums, out_shape=parts, in_specs=hbm(4), out_specs=vme...  2.61 us

profile of v1, /device:TPU:1, one launch (start us, length us, event | category | flops | bytes accessed | tf_op | source)
XLA Modules:
  0.0 106.8 jit_solution(11588275039330244519)
XLA Ops:
  0.0 0.8 copy-done.5
  0.8 0.8 copy-done.7
  1.7 2.6 %slot_sums.1 = bf16[4,128,512]{2,1,0:T(8,128)(2,1)S(1)} custom-call(bf16[256,128]{1,0:T(8,128)(2,1)S(1)} %bitcast.36, bf16[256,128]{1,0:T(8,128)(2,1)S(1)} %bitcast.38, bf16[256,1024]{1,0:T(8,128)(2,1)} %bitcast.22, bf16[256,1024]{1,0:T(8,128)(2,1)} %bitcast.24), custom_call_target="tpu_custom_call" | custom-call | tf_op jit(solution)/shard_map/slot_sums/pallas_call | solution.py:163
  4.3 8.7 %all-gather = bf16[4,1,128,512]{3,2,1,0:T(8,128)(2,1)S(1)} all-gather(bf16[2,1,128,512]{3,2,1,0:T(8,128)(2,1)S(1)} %constant_dynamic-slice_fusion.1), channel_id=2, replica_groups=mesh['x_lo'=2,'core'=2,'y'=4,'x_hi'=2,'z'=16] {'core'}, dimensions={0}, use_global_device_ids=true | all-gather | bytes 786432 | tf_op jit(solution)/shard_map/all_gather | solution.py:130
  13.1 0.0 copy-start.3
  13.1 5.5 %all-gather.1 = bf16[2,1,128,512]{3,2,1,0:T(8,128)(2,1)S(1)} all-gather(bf16[1,1,128,512]{3,2,1,0:T(8,128)(2,1)S(1)} %add_convert_fusion.3), channel_id=3, replica_groups=mesh['x_lo'=2,'core'=2,'y'=4,'x_hi'=2,'z'=16] {'x_lo'}, dimensions={0}, use_global_device_ids=true | all-gather | bytes 393216 | tf_op jit(solution)/shard_map/all_gather | solution.py:138
  18.6 0.1 add_convert_fusion.1
  18.7 33.6 %all_to_all.10 = bf16[128,4,128]{2,1,0:T(4,128)(2,1)S(1)} all-to-all(bf16[128,4,128]{2,1,0:T(4,128)(2,1)S(1)} %reshape.131), channel_id=1, replica_groups=mesh['x_lo'=2,'core'=2,'y'=4,'x_hi'=2,'z'=16] {'y','x_hi','z'}, dimensions={0} | all-to-all | bytes 262144 | tf_op jit(solution)/shard_map/all_to_all | solution.py:150
  52.3 0.1 all_gather_reshape.3
  52.4 9.9 %all_gather.32.rows_ref = bf16[4,128,512]{2,1,0:T(8,128)(2,1)S(1)} all-gather(bf16[1,128,512]{2,1,0:T(8,128)(2,1)S(1)} %all_gather_reshape.3), channel_id=1, replica_groups=mesh['x_lo'=2,'core'=2,'y'=4,'x_hi'=2,'z'=16] {'x_lo','core'}, dimensions={0}, use_global_device_ids=true | all-gather | bytes 655360 | tf_op jit(solution)/shard_map/all_gather | solution.py:181
  62.3 0.0 copy-done.2
  62.3 1.2 %expert.1 = bf16[4,128,512]{2,1,0:T(8,128)(2,1)S(1)} custom-call(bf16[4,128,512]{2,1,0:T(8,128)(2,1)S(1)} %all_gather.32.rows_ref, bf16[1024,512]{1,0:T(8,128)(2,1)S(1)} %bitcast.33, bf16[512,1024]{1,0:T(8,128)(2,1)S(1)} %bitcast.34), custom_call_target="tpu_custom_call" | custom-call | tf_op jit(solution)/shard_map/expert/pallas_call | solution.py:183
  63.6 2.2 %all-gather.2 = bf16[4,1,128,512]{3,2,1,0:T(8,128)(2,1)S(1)} all-gather(bf16[2,1,128,512]{3,2,1,0:T(8,128)(2,1)S(1)} %constant_dynamic-slice_fusion), channel_id=4, replica_groups=mesh['x_lo'=2,'core'=2,'y'=4,'x_hi'=2,'z'=16] {'core'}, dimensions={0}, use_global_device_ids=true | all-gather | bytes 786432 | tf_op jit(solution)/shard_map/all_gather | solution.py:130
  65.8 5.6 %all-gather.3 = bf16[2,1,128,512]{3,2,1,0:T(8,128)(2,1)S(1)} all-gather(bf16[1,1,128,512]{3,2,1,0:T(8,128)(2,1)S(1)} %add_convert_fusion.2), channel_id=5, replica_groups=mesh['x_lo'=2,'core'=2,'y'=4,'x_hi'=2,'z'=16] {'x_lo'}, dimensions={0}, use_global_device_ids=true | all-gather | bytes 393216 | tf_op jit(solution)/shard_map/all_gather | solution.py:138
  71.4 0.1 add_convert_fusion
  71.5 0.0 copy-start.8
  71.5 22.8 %all_to_all.11 = bf16[128,4,128]{2,1,0:T(4,128)(2,1)S(1)} all-to-all(bf16[128,4,128]{2,1,0:T(4,128)(2,1)S(1)} %reshape.132), channel_id=1, replica_groups=mesh['x_lo'=2,'core'=2,'y'=4,'x_hi'=2,'z'=16] {'y','x_hi','z'}, dimensions={0} | all-to-all | bytes 262144 | tf_op jit(solution)/shard_map/all_to_all | solution.py:150
  94.4 0.0 copy-start
  94.4 0.0 copy-start.1
  94.4 0.2 with_totals.1
  94.5 10.6 %all-gather.4 = bf16[576,512]{1,0:T(8,128)(2,1)S(1)} all-gather(bf16[144,512]{1,0:T(8,128)(2,1)S(1)} %with_totals.1), channel_id=6, replica_groups=mesh['x_lo'=2,'core'=2,'y'=4,'x_hi'=2,'z'=16] {'x_lo','core'}, dimensions={0}, use_global_device_ids=true | all-gather | bytes 737280 | tf_op jit(solution)/shard_map/all_gather | solution.py:201
  105.2 0.0 copy-done
  105.2 0.0 copy-done.1
  105.2 1.6 %tokens_back.1 = bf16[256,1024]{1,0:T(8,128)(2,1)} custom-call(bf16[4,144,512]{2,1,0:T(8,128)(2,1)S(1)} %bitcast.21, bf16[256,1024]{1,0:T(8,128)(2,1)S(1)} %bitcast.23, bf16[256,1024]{1,0:T(8,128)(2,1)S(1)} %bitcast.25, bf16[256,128]{1,0:T(8,128)(2,1)S(1)} %bitcast.37, bf16[256,128]{1,0:T(8,128)(2,1)S(1)} %bitcast.39, bf16[1024,128]{1,0:T(8,128)(2,1)S(1)} %copy-done.4), custom_call_target="tpu_custom_call" | custom-call | tf_op jit(solution)/shard_map/tokens_back/pallas_call | solution.py:203
  (16 shorter events, 0.2 us)
Async XLA Ops:
  0.0 0.8 copy-start.5
  0.8 0.8 copy-start.7
  13.1 49.3 %copy-start.3 = (bf16[1,512,1024]{2,1,0:T(8,128)(2,1)S(1)}, bf16[1,512,1024]{2,1,0:T(8,128)(2,1)}, u32[]{:S(2)}) copy-start(bf16[1,512,1024]{2,1,0:T(8,128)(2,1)} %param.12) | copy-start | bytes 3145732
  18.6 43.7 %copy-start.2 = (bf16[1,1024,512]{2,1,0:T(8,128)(2,1)S(1)}, bf16[1,1024,512]{2,1,0:T(8,128)(2,1)}, u32[]{:S(2)}) copy-start(bf16[1,1024,512]{2,1,0:T(8,128)(2,1)} %param.11) | copy-start | bytes 3145732
  71.5 33.6 %copy-start.8 = (bf16[1,256,128]{2,1,0:T(8,128)(2,1)S(1)}, bf16[1,256,128]{2,1,0:T(8,128)(2,1)}, u32[]{:S(2)}) copy-start(bf16[1,256,128]{2,1,0:T(8,128)(2,1)} %param.10) | copy-start | bytes 196612
  94.3 10.8 %copy-start.4 = (bf16[1024,128]{1,0:T(8,128)(2,1)S(1)}, bf16[1024,128]{1,0:T(8,128)(2,1)}, u32[]{:S(2)}) copy-start(bf16[1024,128]{1,0:T(8,128)(2,1)} %keys_ref.1) | copy-start | bytes 786436
  94.4 10.8 %copy-start = (bf16[1,256,1024]{2,1,0:T(8,128)(2,1)S(1)}, bf16[1,256,1024]{2,1,0:T(8,128)(2,1)}, u32[]{:S(2)}) copy-start(bf16[1,256,1024]{2,1,0:T(8,128)(2,1)} %param.7) | copy-start | bytes 1572868
  94.4 10.8 %copy-start.1 = (bf16[1,256,1024]{2,1,0:T(8,128)(2,1)S(1)}, bf16[1,256,1024]{2,1,0:T(8,128)(2,1)}, u32[]{:S(2)}) copy-start(bf16[1,256,1024]{2,1,0:T(8,128)(2,1)} %param.8) | copy-start | bytes 1572868
  94.5 10.6 %copy-start.6 = (bf16[1,256,128]{2,1,0:T(8,128)(2,1)S(1)}, bf16[1,256,128]{2,1,0:T(8,128)(2,1)}, u32[]{:S(2)}) copy-start(bf16[1,256,128]{2,1,0:T(8,128)(2,1)} %param.9) | copy-start | bytes 196612

commit v2 on v1

--- a/solution.py
+++ b/solution.py
@@ -16,27 +16,17 @@
     return lax.dot_general(a, b, (dims, ((), ())), preferred_element_type=F32)
 
 
-def slot_sums(disp_hbm, comb_hbm, tok_hbm, up_hbm, out_ref, disp_ref, comb_ref, tok_ref, up_ref, sems):
+def opening(out_ref):
+    out_ref[...] = jnp.zeros_like(out_ref)
+
+
+def slot_sums(_, disp_ref, comb_ref, tok_ref, up_ref, out_ref):
     quarters, _, both = out_ref.shape
     width = both // 2
-    inputs = ((disp_hbm, disp_ref, tok_hbm, tok_ref), (comb_hbm, comb_ref, up_hbm, up_ref))
-    copies = []
-    for k, (weight_hbm, weight_ref, _, _) in enumerate(inputs):
-        copies.append(pltpu.make_async_copy(weight_hbm, weight_ref, sems.at[quarters, k]))
-    for q in range(quarters):
-        cols = pl.ds(q * width, width)
-        for k, (_, _, src, dst) in enumerate(inputs):
-            copies.append(pltpu.make_async_copy(src.at[:, cols], dst.at[:, cols], sems.at[q, k]))
-    for copy in copies:
-        copy.start()
-    weights = []
-    for k in range(2):
-        copies[k].wait()
-        weights.append(inputs[k][1][...].T)
-    for q in range(quarters):
-        for k, (_, _, _, src) in enumerate(inputs):
-            copies[2 + 2 * q + k].wait()
-            part = dot(weights[k], src[:, q * width : (q + 1) * width], ((1,), (0,)))
+    for k, (weight, src) in enumerate(((disp_ref, tok_ref), (comb_ref, up_ref))):
+        weight = weight[...].T
+        for q in range(quarters):
+            part = dot(weight, src[:, q * width : (q + 1) * width], ((1,), (0,)))
             out_ref[q, :, k * width : (k + 1) * width] = part.astype(BF16)
 
 
@@ -67,11 +57,28 @@
         out_ref[q, :, width:] = dot(pre_grad, first_ref[cols, :], ((1,), (1,))).astype(BF16)
 
 
+def transposed_rows(rows, inner):
+    outer = rows // inner
+    to = lax.broadcasted_iota(jnp.int32, (rows, rows), 0)
+    at = lax.broadcasted_iota(jnp.int32, (rows, rows), 1)
+    return (at == (to % outer) * inner + to // outer).astype(BF16)
+
+
+def plane_sum(rows_ref, out_ref):
+    rows = out_ref.shape[0]
+    order = transposed_rows(rows, 16)
+    total = dot(order, rows_ref[:rows, :], ((1,), (0,)))
+    total += dot(order, rows_ref[rows:, :], ((1,), (0,)))
+    out_ref[...] = total.astype(BF16)
+
+
 def with_totals(back_ref, slots_ref, out_ref):
     rows, both = back_ref.shape
     width = both // 2
-    out_ref[:rows, :] = back_ref[...]
-    product = slots_ref[:, :width].astype(F32) * back_ref[:, width:].astype(F32)
+    order = transposed_rows(rows, rows // 16)
+    back = dot(order, back_ref[...], ((1,), (0,)))
+    out_ref[:rows, :] = back.astype(BF16)
+    product = slots_ref[:, :width].astype(F32) * back[:, width:]
     high = product.astype(BF16)
     low = (product - high.astype(F32)).astype(BF16)
     ones = jnp.ones((16, width), BF16)
@@ -116,28 +123,28 @@
     return [pl.BlockSpec(memory_space=VMEM)] * count
 
 
-def hbm(count):
-    return [pl.BlockSpec(memory_space=pltpu.HBM)] * count
-
-
 def params(mib):
     return pltpu.CompilerParams(vmem_limit_bytes=mib * MIB)
 
 
+def pick(value, at, dim=0):
+    return lax.dynamic_index_in_dim(value, at, dim, keepdims=False)
+
+
+def core_terms(parts, core):
+    given = pick(parts, 1 - core, 1)
+    arrived = lax.all_gather(given, "core", axis=0)
+    return pick(parts, core, 1), pick(arrived, 1 - core)
+
+
 def tok_sum(parts, xl, core):
-    given = lax.dynamic_index_in_dim(parts, 1 - core, 1, keepdims=False)
-    kept = lax.dynamic_index_in_dim(parts, core, 1, keepdims=False)
-    arrived = lax.all_gather(given, "core", axis=0)
-    arrived = lax.dynamic_index_in_dim(arrived, 1 - core, 0, keepdims=False)
+    terms = core_terms(parts, core)
 
     def half(at):
-        return sum(
-            lax.dynamic_index_in_dim(v, at, 0, keepdims=False).astype(F32) for v in (kept, arrived)
-        )
+        return sum(pick(v, at).astype(F32) for v in terms)
 
     across = lax.all_gather(half(1 - xl).astype(BF16), "x_lo", axis=0)
-    across = lax.dynamic_index_in_dim(across, 1 - xl, 0, keepdims=False)
-    return half(xl) + across.astype(F32)
+    return half(xl) + pick(across, 1 - xl).astype(F32)
 
 
 EXP = ("y", "x_hi", "z")
@@ -160,21 +167,22 @@
     xl, core = lax.axis_index("x_lo"), lax.axis_index("core")
     parts = jax.ShapeDtypeStruct((quarters, slots, both), BF16)
 
+    opened = pl.pallas_call(
+        opening,
+        out_shape=jax.ShapeDtypeStruct((8, 128), F32),
+        out_specs=vmem(1)[0],
+        compiler_params=params(1),
+        cost_estimate=pl.CostEstimate(flops=10**10, bytes_accessed=10**7, transcendentals=0),
+        name="opening",
+    )()
     partial = pl.pallas_call(
         slot_sums,
         out_shape=parts,
-        in_specs=hbm(4),
-        out_specs=vmem(1)[0],
-        scratch_shapes=[
-            VMEM((rows, slots), BF16),
-            VMEM((rows, slots), BF16),
-            VMEM((rows, features), BF16),
-            VMEM((rows, features), BF16),
-            pltpu.SemaphoreType.DMA((quarters + 1, 2)),
-        ],
-        compiler_params=params(53),
+        in_specs=vmem(5),
+        out_specs=vmem(1)[0],
+        compiler_params=params(8),
         name="slot_sums",
-    )(dispatch, combine, tokens, upstream)
+    )(opened, dispatch, combine, tokens, upstream)
     summed = tok_sum(partial.reshape(2, 2, slots, both), xl, core).astype(BF16)
     arrived = exchanged(summed)
     images = arrived.shape[0]
@@ -188,8 +196,20 @@
         compiler_params=params(12),
         name="expert",
     )(arrived, w_in[0], w_out[0])
-    leaving = tok_sum(leaving.reshape(2, 2, images, both), xl, core).astype(BF16)
-    returned = exchanged(leaving)
+    terms = core_terms(leaving.reshape(2, 2, images, both), core)
+    leaving = sum(v.astype(F32) for v in terms).astype(BF16)
+    plane = ("x_lo", "y", "x_hi")
+    leaving = lax.all_to_all(leaving.reshape(16, 16, both), plane, 0, 0, tiled=True)
+    leaving = pl.pallas_call(
+        plane_sum,
+        out_shape=jax.ShapeDtypeStruct((slots, both), BF16),
+        in_specs=vmem(1),
+        out_specs=vmem(1)[0],
+        compiler_params=params(4),
+        name="plane_sum",
+    )(leaving.reshape(2 * slots, both))
+    leaving = leaving.reshape(16, slots // 16, both)
+    returned = lax.all_to_all(leaving, "z", 0, 0, tiled=True).reshape(slots, both)
     returned = pl.pallas_call(
         with_totals,
         out_shape=jax.ShapeDtypeStruct((slots + 16, both), BF16),
@@ -204,7 +224,7 @@
         tokens_back,
         out_shape=jax.ShapeDtypeStruct((rows, features), BF16),
         in_specs=vmem(6),
-        out_specs=hbm(1)[0],
+        out_specs=pl.BlockSpec(memory_space=pl.ANY),
         scratch_shapes=[VMEM((rows, features), BF16), pltpu.SemaphoreType.DMA((quarters,))],
         compiler_params=params(12),
         name="tokens_back",

time: 107 us -> 102 us (0.953)
  blocking collectives: 99 us -> 95.6 us
  Pallas kernels: 5.59 us -> 3.65 us
    all_to_all x0 -> x2, blocking collectives: none -> 25.1 us  [the longest x1 14.6 us: body(): lax.all_to_all(leaving, 'z', 0, 0, tiled=True).reshape(slots, both)]
    all_to_all x2 -> x1, blocking collectives: 56.4 us -> 33.7 us  [exchanged(): lax.all_to_all(blocks, EXP, split_axis=0, concat_axis=0, tiled=True)]
    all_gather x2 -> x1, blocking collectives: 11.1 us -> 5.52 us  [tok_sum(): across = lax.all_gather(half(1 - xl).astype(BF16), 'x_lo', axis=0)]
    pallas_call x1 -> x3, Pallas kernels: 2.61 us -> 0.54 us  [the longest x1 0.33 us: body(): pl.pallas_call(slot_sums, out_shape=parts, in_specs=vmem(5), out_specs=vm...]
where the time goes in v2:
time: 102 us
  blocking collectives  95.6 us (94%)
  Pallas kernels  3.65 us (4%)
  local copies, waits for them, and re-layouts  2.25 us (2%)
    all_to_all x1, blocking collectives, exchanged(): lax.all_to_all(blocks, EXP, split_axis=0, concat_axis=0, tiled=True)  33.7 us
    all_to_all x1, blocking collectives, body(): lax.all_to_all(leaving, 'z', 0, 0, tiled=True).reshape(slots, both)  14.6 us
    all_gather x2, blocking collectives, core_terms(): arrived = lax.all_gather(given, 'core', axis=0)  10.9 us
    all_to_all x1, blocking collectives, body(): lax.all_to_all(leaving.reshape(16, 16, both), plane, 0, 0, tiled=True)  10.5 us
    all_gather x1, blocking collectives, body(): returned = lax.all_gather(returned, TOK, axis=0)  10.4 us
    all_gather x1, blocking collectives, body(): arrived = lax.all_gather(arrived, TOK, axis=0)  9.95 us
    all_gather x1, blocking collectives, tok_sum(): across = lax.all_gather(half(1 - xl).astype(BF16), 'x_lo', axis=0)  5.52 us

profile of v2, /device:TPU:1, one launch (start us, length us, event | category | flops | bytes accessed | tf_op | source)
XLA Modules:
  0.0 101.8 jit_solution(14405380121679471091)
XLA Ops:
  0.0 0.0 copy-start.6
  0.1 1.0 copy-done
  1.0 0.2 copy-done.1
  1.2 0.0 copy-done.5
  1.2 0.0 copy-done.6
  1.2 0.3 slot_sums.1
  1.6 8.7 %all-gather = bf16[4,1,128,512]{3,2,1,0:T(8,128)(2,1)S(1)} all-gather(bf16[2,1,128,512]{3,2,1,0:T(8,128)(2,1)S(1)} %constant_dynamic-slice_fusion.2), channel_id=2, replica_groups=mesh['x_lo'=2,'core'=2,'y'=4,'x_hi'=2,'z'=16] {'core'}, dimensions={0}, use_global_device_ids=true | all-gather | bytes 786432 | tf_op jit(solution)/shard_map/all_gather | solution.py:136
  10.3 0.0 copy-start.3
  10.3 5.5 %all-gather.1 = bf16[2,1,128,512]{3,2,1,0:T(8,128)(2,1)S(1)} all-gather(bf16[1,1,128,512]{3,2,1,0:T(8,128)(2,1)S(1)} %add_convert_fusion.1), channel_id=3, replica_groups=mesh['x_lo'=2,'core'=2,'y'=4,'x_hi'=2,'z'=16] {'x_lo'}, dimensions={0}, use_global_device_ids=true | all-gather | bytes 393216 | tf_op jit(solution)/shard_map/all_gather | solution.py:146
  15.8 0.1 add_convert_fusion
  15.9 33.7 %all_to_all.15 = bf16[128,4,128]{2,1,0:T(4,128)(2,1)} all-to-all(bf16[128,4,128]{2,1,0:T(4,128)(2,1)S(1)} %reshape.95), channel_id=1, replica_groups=mesh['x_lo'=2,'core'=2,'y'=4,'x_hi'=2,'z'=16] {'y','x_hi','z'}, dimensions={0} | all-to-all | bytes 262144 | tf_op jit(solution)/shard_map/all_to_all | solution.py:157
  49.7 1.0 all_gather_reshape.3
  50.6 9.9 %all_gather.28.rows_ref = bf16[4,128,512]{2,1,0:T(8,128)(2,1)S(1)} all-gather(bf16[1,128,512]{2,1,0:T(8,128)(2,1)S(1)} %all_gather_reshape.3), channel_id=1, replica_groups=mesh['x_lo'=2,'core'=2,'y'=4,'x_hi'=2,'z'=16] {'x_lo','core'}, dimensions={0}, use_global_device_ids=true | all-gather | bytes 655360 | tf_op jit(solution)/shard_map/all_gather | solution.py:189
  60.6 0.0 copy-done.3
  60.6 0.0 copy-done.2
  60.6 1.2 %expert.1 = bf16[4,128,512]{2,1,0:T(8,128)(2,1)S(1)} custom-call(bf16[4,128,512]{2,1,0:T(8,128)(2,1)S(1)} %all_gather.28.rows_ref, bf16[1024,512]{1,0:T(8,128)(2,1)S(1)} %bitcast.32, bf16[512,1024]{1,0:T(8,128)(2,1)S(1)} %bitcast.33), custom_call_target="tpu_custom_call" | custom-call | tf_op jit(solution)/shard_map/expert/pallas_call | solution.py:191
  61.9 2.2 %all-gather.2 = bf16[4,1,128,512]{3,2,1,0:T(8,128)(2,1)S(1)} all-gather(bf16[2,1,128,512]{3,2,1,0:T(8,128)(2,1)S(1)} %get-tuple-element.6), channel_id=4, replica_groups=mesh['x_lo'=2,'core'=2,'y'=4,'x_hi'=2,'z'=16] {'core'}, dimensions={0}, use_global_device_ids=true | all-gather | bytes 786432 | tf_op jit(solution)/shard_map/all_gather | solution.py:136
  64.1 0.1 fusion
  64.2 10.5 %all_to_all.16 = bf16[16,16,512]{2,1,0:T(8,128)(2,1)S(1)} all-to-all(bf16[16,16,512]{2,1,0:T(8,128)(2,1)S(1)} %fusion), channel_id=1, replica_groups=mesh['x_lo'=2,'core'=2,'y'=4,'x_hi'=2,'z'=16] {'x_lo','y','x_hi'}, dimensions={0} | all-to-all | bytes 524288 | tf_op jit(solution)/shard_map/all_to_all | solution.py:202
  74.6 0.2 plane_sum.1
  74.9 14.6 %all_to_all.17 = bf16[16,8,512]{2,1,0:T(8,128)(2,1)S(1)} all-to-all(bf16[16,8,512]{2,1,0:T(8,128)(2,1)S(1)} %bitcast.36), channel_id=1, replica_groups=mesh['x_lo'=2,'core'=2,'y'=4,'x_hi'=2,'z'=16] {'z'}, dimensions={0} | all-to-all | bytes 262144 | tf_op jit(solution)/shard_map/all_to_all | solution.py:212
  89.5 0.3 with_totals.1
  89.8 10.4 %all-gather.3 = bf16[576,512]{1,0:T(8,128)(2,1)S(1)} all-gather(bf16[144,512]{1,0:T(8,128)(2,1)S(1)} %with_totals.1), channel_id=5, replica_groups=mesh['x_lo'=2,'core'=2,'y'=4,'x_hi'=2,'z'=16] {'x_lo','core'}, dimensions={0}, use_global_device_ids=true | all-gather | bytes 737280 | tf_op jit(solution)/shard_map/all_gather | solution.py:221
  100.2 1.6 %tokens_back.1 = bf16[256,1024]{1,0:T(8,128)(2,1)} custom-call(bf16[4,144,512]{2,1,0:T(8,128)(2,1)S(1)} %bitcast.22, bf16[256,1024]{1,0:T(8,128)(2,1)S(1)} %bitcast.24, bf16[256,1024]{1,0:T(8,128)(2,1)S(1)} %bitcast.26, bf16[256,128]{1,0:T(8,128)(2,1)S(1)} %bitcast.38, bf16[256,128]{1,0:T(8,128)(2,1)S(1)} %bitcast.40, bf16[1024,128]{1,0:T(8,128)(2,1)S(1)} %copy-done.4), custom_call_target="tpu_custom_call" | custom-call | tf_op jit(solution)/shard_map/tokens_back/pallas_call | solution.py:223
  (12 shorter events, 0.2 us)
Async XLA Ops:
  0.0 1.0 %copy-start = (bf16[1,256,1024]{2,1,0:T(8,128)(2,1)S(1)}, bf16[1,256,1024]{2,1,0:T(8,128)(2,1)}, u32[]{:S(2)}) copy-start(bf16[1,256,1024]{2,1,0:T(8,128)(2,1)} %param.7) | copy-start | bytes 1572868
  0.0 1.2 %copy-start.1 = (bf16[1,256,1024]{2,1,0:T(8,128)(2,1)S(1)}, bf16[1,256,1024]{2,1,0:T(8,128)(2,1)}, u32[]{:S(2)}) copy-start(bf16[1,256,1024]{2,1,0:T(8,128)(2,1)} %param.8) | copy-start | bytes 1572868
  0.0 1.2 %copy-start.5 = (bf16[1,256,128]{2,1,0:T(8,128)(2,1)S(1)}, bf16[1,256,128]{2,1,0:T(8,128)(2,1)}, u32[]{:S(2)}) copy-start(bf16[1,256,128]{2,1,0:T(8,128)(2,1)} %param.9) | copy-start | bytes 196612
  0.0 1.2 %copy-start.6 = (bf16[1,256,128]{2,1,0:T(8,128)(2,1)S(1)}, bf16[1,256,128]{2,1,0:T(8,128)(2,1)}, u32[]{:S(2)}) copy-start(bf16[1,256,128]{2,1,0:T(8,128)(2,1)} %param.10) | copy-start | bytes 196612
  10.3 50.3 %copy-start.3 = (bf16[1,512,1024]{2,1,0:T(8,128)(2,1)S(1)}, bf16[1,512,1024]{2,1,0:T(8,128)(2,1)}, u32[]{:S(2)}) copy-start(bf16[1,512,1024]{2,1,0:T(8,128)(2,1)} %param.12) | copy-start | bytes 3145732
  15.8 44.8 %copy-start.2 = (bf16[1,1024,512]{2,1,0:T(8,128)(2,1)S(1)}, bf16[1,1024,512]{2,1,0:T(8,128)(2,1)}, u32[]{:S(2)}) copy-start(bf16[1,1024,512]{2,1,0:T(8,128)(2,1)} %param.11) | copy-start | bytes 3145732
  89.8 10.4 %copy-start.4 = (bf16[1024,128]{1,0:T(8,128)(2,1)S(1)}, bf16[1024,128]{1,0:T(8,128)(2,1)}, u32[]{:S(2)}) copy-start(bf16[1024,128]{1,0:T(8,128)(2,1)} %keys_ref.1) | copy-start | bytes 786436

commit v3 on v2

--- a/solution.py
+++ b/solution.py
@@ -40,28 +40,30 @@
     return gelu_value, gelu_slope
 
 
-def expert(rows_ref, first_ref, second_ref, out_ref):
-    quarters, _, both = rows_ref.shape
-    width = both // 2
-    pre_act = hidden_grad = 0.0
-    for q in range(quarters):
-        cols = slice(q * width, (q + 1) * width)
-        pre_act += dot(rows_ref[q, :, :width], first_ref[cols, :], ((1,), (0,)))
-        hidden_grad += dot(rows_ref[q, :, width:], second_ref[:, cols], ((1,), (1,)))
-    value, slope = gelu_parts(pre_act)
-    hidden = value.astype(BF16)
-    pre_grad = (hidden_grad * slope).astype(BF16)
-    for q in range(quarters):
-        cols = slice(q * width, (q + 1) * width)
-        out_ref[q, :, :width] = dot(hidden, second_ref[:, cols], ((1,), (0,))).astype(BF16)
-        out_ref[q, :, width:] = dot(pre_grad, first_ref[cols, :], ((1,), (1,))).astype(BF16)
-
-
 def transposed_rows(rows, inner):
     outer = rows // inner
     to = lax.broadcasted_iota(jnp.int32, (rows, rows), 0)
     at = lax.broadcasted_iota(jnp.int32, (rows, rows), 1)
     return (at == (to % outer) * inner + to // outer).astype(BF16)
+
+
+def expert(rows_ref, first_ref, second_ref, out_ref):
+    quarters, images, both = out_ref.shape
+    width = both // 2
+    order = transposed_rows(images, images // 16)
+    pre_act = hidden_grad = 0.0
+    for q in range(quarters):
+        cols = slice(q * width, (q + 1) * width)
+        rows = dot(order, rows_ref[q, :, :both], ((1,), (0,))).astype(BF16)
+        pre_act += dot(rows[:, :width], first_ref[cols, :], ((1,), (0,)))
+        hidden_grad += dot(rows[:, width:], second_ref[:, cols], ((1,), (1,)))
+    value, slope = gelu_parts(pre_act)
+    hidden = value.astype(BF16)
+    pre_grad = (hidden_grad * slope).astype(BF16)
+    for q in range(quarters):
+        cols = slice(q * width, (q + 1) * width)
+        out_ref[q, :, :width] = dot(hidden, second_ref[:, cols], ((1,), (0,))).astype(BF16)
+        out_ref[q, :, width:] = dot(pre_grad, first_ref[cols, :], ((1,), (1,))).astype(BF16)
 
 
 def plane_sum(rows_ref, out_ref):
@@ -78,7 +80,7 @@
     order = transposed_rows(rows, rows // 16)
     back = dot(order, back_ref[...], ((1,), (0,)))
     out_ref[:rows, :] = back.astype(BF16)
-    product = slots_ref[:, :width].astype(F32) * back[:, width:]
+    product = slots_ref[...] * back[:, width:]
     high = product.astype(BF16)
     low = (product - high.astype(F32)).astype(BF16)
     ones = jnp.ones((16, width), BF16)
@@ -131,30 +133,32 @@
     return lax.dynamic_index_in_dim(value, at, dim, keepdims=False)
 
 
-def core_terms(parts, core):
-    given = pick(parts, 1 - core, 1)
-    arrived = lax.all_gather(given, "core", axis=0)
-    return pick(parts, core, 1), pick(arrived, 1 - core)
-
-
-def tok_sum(parts, xl, core):
-    terms = core_terms(parts, core)
-
-    def half(at):
-        return sum(pick(v, at).astype(F32) for v in terms)
-
-    across = lax.all_gather(half(1 - xl).astype(BF16), "x_lo", axis=0)
-    return half(xl) + pick(across, 1 - xl).astype(F32)
-
-
+TOK = ("x_lo", "core")
+PLANE = ("x_lo", "y", "x_hi")
 EXP = ("y", "x_hi", "z")
-TOK = ("x_lo", "core")
+
+
+def chip_sum(parts, core):
+    parts = parts.reshape(2, 2, *parts.shape[1:])
+    arrived = lax.all_gather(pick(parts, 1 - core, 1), "core", axis=0)
+    terms = (pick(parts, core, 1), pick(arrived, 1 - core))
+    return sum(v.astype(F32) for v in terms).astype(BF16)
 
 
 def exchanged(value):
-    rows, cols = value.shape
-    blocks = value.reshape(rows, cols // 128, 128)
-    return lax.all_to_all(blocks, EXP, split_axis=0, concat_axis=0, tiled=True).reshape(rows, cols)
+    halves, rows, both = value.shape
+    value = value.reshape(halves * rows // 16, 16, both)
+    value = lax.all_to_all(value, PLANE, 0, 0, tiled=True)
+    value = pl.pallas_call(
+        plane_sum,
+        out_shape=jax.ShapeDtypeStruct((rows, both), BF16),
+        in_specs=vmem(1),
+        out_specs=vmem(1)[0],
+        compiler_params=params(4),
+        name="plane_sum",
+    )(value.reshape(halves * rows, both))
+    value = value.reshape(16, rows // 16, both)
+    return lax.all_to_all(value, "z", 0, 0, tiled=True).reshape(rows, both)
 
 
 def body(tokens, upstream, dispatch, combine, w_in, w_out, slot_keys):
@@ -164,7 +168,9 @@
     quarters = 4
     width = features // quarters
     both = 2 * width
-    xl, core = lax.axis_index("x_lo"), lax.axis_index("core")
+    xl, core = (lax.axis_index(axis).astype(jnp.uint32) for axis in TOK)
+    partner = 2 * (1 - xl) + core
+    across = 1 - xl
     parts = jax.ShapeDtypeStruct((quarters, slots, both), BF16)
 
     opened = pl.pallas_call(
@@ -183,10 +189,16 @@
         compiler_params=params(8),
         name="slot_sums",
     )(opened, dispatch, combine, tokens, upstream)
-    summed = tok_sum(partial.reshape(2, 2, slots, both), xl, core).astype(BF16)
-    arrived = exchanged(summed)
+    held = (partial, xl, across, core, partner)
+    partial, xl, across, core, partner = lax.optimization_barrier(held)
+    sums = lax.optimization_barrier(chip_sum(partial, core))
+    arrived, sums = lax.optimization_barrier((exchanged(sums), sums))
     images = arrived.shape[0]
-    arrived = lax.all_gather(arrived, TOK, axis=0)
+    spare = pick(sums, across)[:, :width]
+    arrived = lax.all_gather(jnp.concatenate([arrived, spare], axis=1), TOK, axis=0)
+    other = pick(arrived, partner)[:, both:]
+    slot_input = pick(sums, xl)[:, :width].astype(F32) + other.astype(F32)
+    arrived, slot_input = lax.optimization_barrier((arrived, slot_input))
 
     leaving = pl.pallas_call(
         expert,
@@ -196,20 +208,7 @@
         compiler_params=params(12),
         name="expert",
     )(arrived, w_in[0], w_out[0])
-    terms = core_terms(leaving.reshape(2, 2, images, both), core)
-    leaving = sum(v.astype(F32) for v in terms).astype(BF16)
-    plane = ("x_lo", "y", "x_hi")
-    leaving = lax.all_to_all(leaving.reshape(16, 16, both), plane, 0, 0, tiled=True)
-    leaving = pl.pallas_call(
-        plane_sum,
-        out_shape=jax.ShapeDtypeStruct((slots, both), BF16),
-        in_specs=vmem(1),
-        out_specs=vmem(1)[0],
-        compiler_params=params(4),
-        name="plane_sum",
-    )(leaving.reshape(2 * slots, both))
-    leaving = leaving.reshape(16, slots // 16, both)
-    returned = lax.all_to_all(leaving, "z", 0, 0, tiled=True).reshape(slots, both)
+    returned = exchanged(chip_sum(leaving, core))
     returned = pl.pallas_call(
         with_totals,
         out_shape=jax.ShapeDtypeStruct((slots + 16, both), BF16),
@@ -217,7 +216,7 @@
         out_specs=vmem(1)[0],
         compiler_params=params(4),
         name="with_totals",
-    )(returned, summed)
+    )(returned, slot_input)
     returned = lax.all_gather(returned, TOK, axis=0)
 
     result = pl.pallas_call(

time: 102 us -> 102 us (level)
    all_gather x4 -> x3, blocking collectives: 26.3 us -> 22.6 us  [the longest x1 11.7 us: body(): lax.all_gather(jnp.concatenate([arrived, spare], axis=1), TOK, axis=0)]
    all_to_all x3 -> x4, blocking collectives: 58.9 us -> 62 us  [the longest x2 40.2 us: exchanged(): return lax.all_to_all(value, 'z', 0, 0, tiled=True).reshape(rows, both)]
where the time goes in v3:
time: 102 us; the launch traced here: 101 us
  blocking collectives  95.4 us (94%)
  Pallas kernels  4.32 us (4%)
  local copies, waits for them, and re-layouts  1.31 us (1%)
    all_to_all x2, blocking collectives, exchanged(): return lax.all_to_all(value, 'z', 0, 0, tiled=True).reshape(rows, both)  40.2 us
    all_to_all x2, blocking collectives, exchanged(): value = lax.all_to_all(value, PLANE, 0, 0, tiled=True)  21.7 us
    all_gather x1, blocking collectives, body(): lax.all_gather(jnp.concatenate([arrived, spare], axis=1), TOK, axis=0)  11.7 us
    all_gather x2, blocking collectives, chip_sum(): arrived = lax.all_gather(pick(parts, 1 - core, 1), 'core', axis=0)  10.9 us
    all_gather x1, blocking collectives, body(): returned = lax.all_gather(returned, TOK, axis=0)  10.8 us

profile of v3, /device:TPU:1, one launch (start us, length us, event | category | flops | bytes accessed | tf_op | source)
XLA Modules:
  0.0 101.3 jit_solution(10531316780188228640)
XLA Ops:
  0.0 0.0 copy-start.6
  0.0 1.0 copy-done
  1.0 0.2 copy-done.1
  1.2 0.0 copy-done.5
  1.2 0.3 slot_sums.1
  1.6 8.7 %all-gather = bf16[4,1,128,512]{3,2,1,0:T(8,128)(2,1)S(1)} all-gather(bf16[2,1,128,512]{3,2,1,0:T(8,128)(2,1)S(1)} %constant_dynamic-slice_fusion.2), channel_id=2, replica_groups=mesh['x_lo'=2,'core'=2,'y'=4,'x_hi'=2,'z'=16] {'core'}, dimensions={0}, use_global_device_ids=true | all-gather | bytes 786432 | tf_op jit(solution)/shard_map/all_gather | solution.py:143
  10.3 0.1 fusion.1
  10.3 10.3 %all_to_all.20 = bf16[16,16,512]{2,1,0:T(8,128)(2,1)S(1)} all-to-all(bf16[16,16,512]{2,1,0:T(8,128)(2,1)S(1)} %bitcast.57), channel_id=1, replica_groups=mesh['x_lo'=2,'core'=2,'y'=4,'x_hi'=2,'z'=16] {'x_lo','y','x_hi'}, dimensions={0} | all-to-all | bytes 524288 | tf_op jit(solution)/shard_map/all_to_all | solution.py:151
  20.6 0.2 plane_sum.2
  20.8 25.4 %all_to_all.21 = bf16[16,8,512]{2,1,0:T(8,128)(2,1)S(1)} all-to-all(bf16[16,8,512]{2,1,0:T(8,128)(2,1)S(1)} %bitcast.51), channel_id=1, replica_groups=mesh['x_lo'=2,'core'=2,'y'=4,'x_hi'=2,'z'=16] {'z'}, dimensions={0} | all-to-all | bytes 262144 | tf_op jit(solution)/shard_map/all_to_all | solution.py:161
  46.2 0.0 copy-start.3
  46.2 0.0 copy-start.2
  46.3 11.7 %all-gather.1 = bf16[512,768]{1,0:T(8,128)(2,1)S(1)} all-gather(bf16[128,768]{1,0:T(8,128)(2,1)S(1)} %pad_maximum_fusion), channel_id=3, replica_groups=mesh['x_lo'=2,'core'=2,'y'=4,'x_hi'=2,'z'=16] {'x_lo','core'}, dimensions={0}, use_global_device_ids=true | all-gather | bytes 983040 | tf_op jit(solution)/shard_map/all_gather | solution.py:198
  58.0 0.0 copy-done.3
  58.0 0.0 copy-done.2
  58.0 1.7 %expert.1 = bf16[4,128,512]{2,1,0:T(8,128)(2,1)S(1)} custom-call(bf16[4,128,768]{2,1,0:T(8,128)(2,1)S(1)} %bitcast.37, bf16[1024,512]{1,0:T(8,128)(2,1)S(1)} %bitcast.46, bf16[512,1024]{1,0:T(8,128)(2,1)S(1)} %bitcast.47), custom_call_target="tpu_custom_call" | custom-call | tf_op jit(solution)/shard_map/expert/pallas_call | solution.py:203
  59.8 2.2 %all-gather.2 = bf16[4,1,128,512]{3,2,1,0:T(8,128)(2,1)S(1)} all-gather(bf16[2,1,128,512]{3,2,1,0:T(8,128)(2,1)S(1)} %get-tuple-element.24), channel_id=4, replica_groups=mesh['x_lo'=2,'core'=2,'y'=4,'x_hi'=2,'z'=16] {'core'}, dimensions={0}, use_global_device_ids=true | all-gather | bytes 786432 | tf_op jit(solution)/shard_map/all_gather | solution.py:143
  62.0 0.1 fusion
  62.1 11.5 %all_to_all.22 = bf16[16,16,512]{2,1,0:T(8,128)(2,1)S(1)} all-to-all(bf16[16,16,512]{2,1,0:T(8,128)(2,1)S(1)} %fusion), channel_id=1, replica_groups=mesh['x_lo'=2,'core'=2,'y'=4,'x_hi'=2,'z'=16] {'x_lo','y','x_hi'}, dimensions={0} | all-to-all | bytes 524288 | tf_op jit(solution)/shard_map/all_to_all | solution.py:151
  73.5 0.2 plane_sum.3
  73.8 14.9 %all_to_all.23 = bf16[16,8,512]{2,1,0:T(8,128)(2,1)S(1)} all-to-all(bf16[16,8,512]{2,1,0:T(8,128)(2,1)S(1)} %bitcast.52), channel_id=1, replica_groups=mesh['x_lo'=2,'core'=2,'y'=4,'x_hi'=2,'z'=16] {'z'}, dimensions={0} | all-to-all | bytes 262144 | tf_op jit(solution)/shard_map/all_to_all | solution.py:161
  88.7 0.3 with_totals.1
  89.0 10.8 %all-gather.3 = bf16[576,512]{1,0:T(8,128)(2,1)S(1)} all-gather(bf16[144,512]{1,0:T(8,128)(2,1)S(1)} %with_totals.1), channel_id=5, replica_groups=mesh['x_lo'=2,'core'=2,'y'=4,'x_hi'=2,'z'=16] {'x_lo','core'}, dimensions={0}, use_global_device_ids=true | all-gather | bytes 737280 | tf_op jit(solution)/shard_map/all_gather | solution.py:220
  99.7 1.6 %tokens_back.1 = bf16[256,1024]{1,0:T(8,128)(2,1)} custom-call(bf16[4,144,512]{2,1,0:T(8,128)(2,1)S(1)} %bitcast.38, bf16[256,1024]{1,0:T(8,128)(2,1)S(1)} %bitcast.40, bf16[256,1024]{1,0:T(8,128)(2,1)S(1)} %bitcast.42, bf16[256,128]{1,0:T(8,128)(2,1)S(1)} %bitcast.54, bf16[256,128]{1,0:T(8,128)(2,1)S(1)} %bitcast.56, bf16[1024,128]{1,0:T(8,128)(2,1)S(1)} %copy-done.4), custom_call_target="tpu_custom_call" | custom-call | tf_op jit(solution)/shard_map/tokens_back/pallas_call | solution.py:222
  (15 shorter events, 0.2 us)
Async XLA Ops:
  0.0 1.0 %copy-start = (bf16[1,256,1024]{2,1,0:T(8,128)(2,1)S(1)}, bf16[1,256,1024]{2,1,0:T(8,128)(2,1)}, u32[]{:S(2)}) copy-start(bf16[1,256,1024]{2,1,0:T(8,128)(2,1)} %param.7) | copy-start | bytes 1572868
  0.0 1.2 %copy-start.1 = (bf16[1,256,1024]{2,1,0:T(8,128)(2,1)S(1)}, bf16[1,256,1024]{2,1,0:T(8,128)(2,1)}, u32[]{:S(2)}) copy-start(bf16[1,256,1024]{2,1,0:T(8,128)(2,1)} %param.8) | copy-start | bytes 1572868
  0.0 1.2 %copy-start.5 = (bf16[1,256,128]{2,1,0:T(8,128)(2,1)S(1)}, bf16[1,256,128]{2,1,0:T(8,128)(2,1)}, u32[]{:S(2)}) copy-start(bf16[1,256,128]{2,1,0:T(8,128)(2,1)} %param.9) | copy-start | bytes 196612
  0.0 1.2 %copy-start.6 = (bf16[1,256,128]{2,1,0:T(8,128)(2,1)S(1)}, bf16[1,256,128]{2,1,0:T(8,128)(2,1)}, u32[]{:S(2)}) copy-start(bf16[1,256,128]{2,1,0:T(8,128)(2,1)} %param.10) | copy-start | bytes 196612
  46.2 11.8 %copy-start.3 = (bf16[1,512,1024]{2,1,0:T(8,128)(2,1)S(1)}, bf16[1,512,1024]{2,1,0:T(8,128)(2,1)}, u32[]{:S(2)}) copy-start(bf16[1,512,1024]{2,1,0:T(8,128)(2,1)} %param.12) | copy-start | bytes 3145732
  46.2 11.8 %copy-start.2 = (bf16[1,1024,512]{2,1,0:T(8,128)(2,1)S(1)}, bf16[1,1024,512]{2,1,0:T(8,128)(2,1)}, u32[]{:S(2)}) copy-start(bf16[1,1024,512]{2,1,0:T(8,128)(2,1)} %param.11) | copy-start | bytes 3145732
  88.9 10.8 %copy-start.4 = (bf16[1024,128]{1,0:T(8,128)(2,1)S(1)}, bf16[1024,128]{1,0:T(8,128)(2,1)}, u32[]{:S(2)}) copy-start(bf16[1024,128]{1,0:T(8,128)(2,1)} %keys_ref.1) | copy-start | bytes 786436

commit v4 on v2

--- a/solution.py
+++ b/solution.py
@@ -186,6 +186,7 @@
     summed = tok_sum(partial.reshape(2, 2, slots, both), xl, core).astype(BF16)
     arrived = exchanged(summed)
     images = arrived.shape[0]
+    arrived, w_in, w_out = lax.optimization_barrier((arrived, w_in, w_out))
     arrived = lax.all_gather(arrived, TOK, axis=0)
 
     leaving = pl.pallas_call(

time: 102 us -> 101 us (level)
  no operation moved by 1% of the time
where the time goes in v4:
time: 101 us
  blocking collectives  95.5 us (95%)
  Pallas kernels  3.66 us (4%)
  local copies, waits for them, and re-layouts  1.31 us (1%)
    all_to_all x1, blocking collectives, exchanged(): lax.all_to_all(blocks, EXP, split_axis=0, concat_axis=0, tiled=True)  33.6 us
    all_to_all x1, blocking collectives, body(): lax.all_to_all(leaving, 'z', 0, 0, tiled=True).reshape(slots, both)  14.6 us
    all_gather x2, blocking collectives, core_terms(): arrived = lax.all_gather(given, 'core', axis=0)  10.9 us
    all_to_all x1, blocking collectives, body(): lax.all_to_all(leaving.reshape(16, 16, both), plane, 0, 0, tiled=True)  10.5 us
    all_gather x1, blocking collectives, body(): returned = lax.all_gather(returned, TOK, axis=0)  10.4 us
    all_gather x1, blocking collectives, body(): arrived = lax.all_gather(arrived, TOK, axis=0)  9.93 us
    all_gather x1, blocking collectives, tok_sum(): across = lax.all_gather(half(1 - xl).astype(BF16), 'x_lo', axis=0)  5.52 us

profile of v4, /device:TPU:1, one launch (start us, length us, event | category | flops | bytes accessed | tf_op | source)
XLA Modules:
  0.0 100.7 jit_solution(7197293895789399728)
XLA Ops:
  0.0 0.0 copy-start.6
  0.1 1.0 copy-done
  1.0 0.2 copy-done.1
  1.2 0.0 copy-done.5
  1.2 0.0 copy-done.6
  1.2 0.3 slot_sums.1
  1.6 8.7 %all-gather = bf16[4,1,128,512]{3,2,1,0:T(8,128)(2,1)S(1)} all-gather(bf16[2,1,128,512]{3,2,1,0:T(8,128)(2,1)S(1)} %constant_dynamic-slice_fusion.2), channel_id=2, replica_groups=mesh['x_lo'=2,'core'=2,'y'=4,'x_hi'=2,'z'=16] {'core'}, dimensions={0}, use_global_device_ids=true | all-gather | bytes 786432 | tf_op jit(solution)/shard_map/all_gather | solution.py:136
  10.3 0.0 copy-start.3
  10.3 5.5 %all-gather.1 = bf16[2,1,128,512]{3,2,1,0:T(8,128)(2,1)S(1)} all-gather(bf16[1,1,128,512]{3,2,1,0:T(8,128)(2,1)S(1)} %add_convert_fusion.1), channel_id=3, replica_groups=mesh['x_lo'=2,'core'=2,'y'=4,'x_hi'=2,'z'=16] {'x_lo'}, dimensions={0}, use_global_device_ids=true | all-gather | bytes 393216 | tf_op jit(solution)/shard_map/all_gather | solution.py:146
  15.8 0.1 add_convert_fusion
  15.9 33.6 %all_to_all.15 = bf16[128,4,128]{2,1,0:T(4,128)(2,1)S(1)} all-to-all(bf16[128,4,128]{2,1,0:T(4,128)(2,1)S(1)} %reshape.100), channel_id=1, replica_groups=mesh['x_lo'=2,'core'=2,'y'=4,'x_hi'=2,'z'=16] {'y','x_hi','z'}, dimensions={0} | all-to-all | bytes 262144 | tf_op jit(solution)/shard_map/all_to_all | solution.py:157
  49.6 9.9 %all-gather.2 = bf16[512,512]{1,0:T(8,128)(2,1)S(1)} all-gather(bf16[128,512]{1,0:T(8,128)(2,1)S(1)} %bitcast.52), channel_id=4, replica_groups=mesh['x_lo'=2,'core'=2,'y'=4,'x_hi'=2,'z'=16] {'x_lo','core'}, dimensions={0}, use_global_device_ids=true | all-gather | bytes 655360 | tf_op jit(solution)/shard_map/all_gather | solution.py:190
  59.5 0.0 copy-done.3
  59.5 0.0 copy-done.2
  59.5 1.2 %expert.1 = bf16[4,128,512]{2,1,0:T(8,128)(2,1)S(1)} custom-call(bf16[4,128,512]{2,1,0:T(8,128)(2,1)S(1)} %bitcast.36, bf16[1024,512]{1,0:T(8,128)(2,1)S(1)} %bitcast.38, bf16[512,1024]{1,0:T(8,128)(2,1)S(1)} %bitcast.39), custom_call_target="tpu_custom_call" | custom-call | tf_op jit(solution)/shard_map/expert/pallas_call | solution.py:192
  60.8 2.2 %all-gather.3 = bf16[4,1,128,512]{3,2,1,0:T(8,128)(2,1)S(1)} all-gather(bf16[2,1,128,512]{3,2,1,0:T(8,128)(2,1)S(1)} %get-tuple-element.12), channel_id=5, replica_groups=mesh['x_lo'=2,'core'=2,'y'=4,'x_hi'=2,'z'=16] {'core'}, dimensions={0}, use_global_device_ids=true | all-gather | bytes 786432 | tf_op jit(solution)/shard_map/all_gather | solution.py:136
  63.0 0.1 fusion
  63.1 10.5 %all_to_all.16 = bf16[16,16,512]{2,1,0:T(8,128)(2,1)S(1)} all-to-all(bf16[16,16,512]{2,1,0:T(8,128)(2,1)S(1)} %fusion), channel_id=1, replica_groups=mesh['x_lo'=2,'core'=2,'y'=4,'x_hi'=2,'z'=16] {'x_lo','y','x_hi'}, dimensions={0} | all-to-all | bytes 524288 | tf_op jit(solution)/shard_map/all_to_all | solution.py:203
  73.6 0.2 plane_sum.1
  73.8 14.6 %all_to_all.17 = bf16[16,8,512]{2,1,0:T(8,128)(2,1)S(1)} all-to-all(bf16[16,8,512]{2,1,0:T(8,128)(2,1)S(1)} %bitcast.42), channel_id=1, replica_groups=mesh['x_lo'=2,'core'=2,'y'=4,'x_hi'=2,'z'=16] {'z'}, dimensions={0} | all-to-all | bytes 262144 | tf_op jit(solution)/shard_map/all_to_all | solution.py:213
  88.5 0.3 with_totals.1
  88.7 10.4 %all-gather.4 = bf16[576,512]{1,0:T(8,128)(2,1)S(1)} all-gather(bf16[144,512]{1,0:T(8,128)(2,1)S(1)} %with_totals.1), channel_id=6, replica_groups=mesh['x_lo'=2,'core'=2,'y'=4,'x_hi'=2,'z'=16] {'x_lo','core'}, dimensions={0}, use_global_device_ids=true | all-gather | bytes 737280 | tf_op jit(solution)/shard_map/all_gather | solution.py:222
  99.1 0.0 copy-done.4
  99.1 1.6 %tokens_back.1 = bf16[256,1024]{1,0:T(8,128)(2,1)} custom-call(bf16[4,144,512]{2,1,0:T(8,128)(2,1)S(1)} %bitcast.27, bf16[256,1024]{1,0:T(8,128)(2,1)S(1)} %bitcast.29, bf16[256,1024]{1,0:T(8,128)(2,1)S(1)} %bitcast.31, bf16[256,128]{1,0:T(8,128)(2,1)S(1)} %bitcast.44, bf16[256,128]{1,0:T(8,128)(2,1)S(1)} %bitcast.46, bf16[1024,128]{1,0:T(8,128)(2,1)S(1)} %copy-done.4), custom_call_target="tpu_custom_call" | custom-call | tf_op jit(solution)/shard_map/tokens_back/pallas_call | solution.py:224
  (12 shorter events, 0.2 us)
Async XLA Ops:
  0.0 1.0 %copy-start = (bf16[1,256,1024]{2,1,0:T(8,128)(2,1)S(1)}, bf16[1,256,1024]{2,1,0:T(8,128)(2,1)}, u32[]{:S(2)}) copy-start(bf16[1,256,1024]{2,1,0:T(8,128)(2,1)} %param.7) | copy-start | bytes 1572868
  0.0 1.2 %copy-start.1 = (bf16[1,256,1024]{2,1,0:T(8,128)(2,1)S(1)}, bf16[1,256,1024]{2,1,0:T(8,128)(2,1)}, u32[]{:S(2)}) copy-start(bf16[1,256,1024]{2,1,0:T(8,128)(2,1)} %param.8) | copy-start | bytes 1572868
  0.0 1.2 %copy-start.5 = (bf16[1,256,128]{2,1,0:T(8,128)(2,1)S(1)}, bf16[1,256,128]{2,1,0:T(8,128)(2,1)}, u32[]{:S(2)}) copy-start(bf16[1,256,128]{2,1,0:T(8,128)(2,1)} %param.9) | copy-start | bytes 196612
  0.0 1.2 %copy-start.6 = (bf16[1,256,128]{2,1,0:T(8,128)(2,1)S(1)}, bf16[1,256,128]{2,1,0:T(8,128)(2,1)}, u32[]{:S(2)}) copy-start(bf16[1,256,128]{2,1,0:T(8,128)(2,1)} %param.10) | copy-start | bytes 196612
  10.3 49.2 %copy-start.3 = (bf16[1,512,1024]{2,1,0:T(8,128)(2,1)S(1)}, bf16[1,512,1024]{2,1,0:T(8,128)(2,1)}, u32[]{:S(2)}) copy-start(bf16[1,512,1024]{2,1,0:T(8,128)(2,1)} %param.12) | copy-start | bytes 3145732
  15.8 43.7 %copy-start.2 = (bf16[1,1024,512]{2,1,0:T(8,128)(2,1)S(1)}, bf16[1,1024,512]{2,1,0:T(8,128)(2,1)}, u32[]{:S(2)}) copy-start(bf16[1,1024,512]{2,1,0:T(8,128)(2,1)} %param.11) | copy-start | bytes 3145732
  88.7 10.4 %copy-start.4 = (bf16[1024,128]{1,0:T(8,128)(2,1)S(1)}, bf16[1024,128]{1,0:T(8,128)(2,1)}, u32[]{:S(2)}) copy-start(bf16[1024,128]{1,0:T(8,128)(2,1)} %keys_ref.1) | copy-start | bytes 786436

commit v5 on v3

v5 whole, which is shorter than its diff:
```python
import jax
import jax.numpy as jnp
from jax import lax
from jax.experimental import pallas as pl
from jax.experimental.pallas import tpu as pltpu
from jax.sharding import Mesh
from jax.sharding import PartitionSpec as P

F32 = jnp.float32
BF16 = jnp.bfloat16
VMEM = pltpu.VMEM
MIB = 1024 * 1024


def dot(a, b, dims):
    return lax.dot_general(a, b, (dims, ((), ())), preferred_element_type=F32)


def opening(out_ref):
    out_ref[...] = jnp.zeros_like(out_ref)


def slot_sums(_, disp_ref, comb_ref, tok_ref, up_ref, out_ref):
    quarters, _, both = out_ref.shape
    width = both // 2
    for k, (weight, src) in enumerate(((disp_ref, tok_ref), (comb_ref, up_ref))):
        weight = weight[...].T
        for q in range(quarters):
            part = dot(weight, src[:, q * width : (q + 1) * width], ((1,), (0,)))
            out_ref[q, :, k * width : (k + 1) * width] = part.astype(BF16)


def gelu_parts(pre_act):
    inside = 0.7978845608 * (pre_act + 0.044715 * pre_act * pre_act * pre_act)
    tanh_val = jnp.tanh(inside)
    gelu_value = 0.5 * pre_act * (1.0 + tanh_val)
    gelu_slope = 0.5 * (1.0 + tanh_val) + 0.5 * pre_act * (
        1.0 - tanh_val * tanh_val
    ) * 0.7978845608 * (1.0 + 3.0 * 0.044715 * pre_act * pre_act)
    return gelu_value, gelu_slope


def expert(place_ref, rows_ref, first_ref, second_ref, out_ref):
    quarters, images, both = rows_ref.shape
    width = both // 2
    pre_act = hidden_grad = total = 0.0
    for q in range(quarters):
        cols = slice(q * width, (q + 1) * width)
        pre_act += dot(rows_ref[q, :, :width], first_ref[cols, :], ((1,), (0,)))
        hidden_grad += dot(rows_ref[q, :, width:], second_ref[:, cols], ((1,), (1,)))
    value, slope = gelu_parts(pre_act)
    hidden = value.astype(BF16)
    pre_grad = (hidden_grad * slope).astype(BF16)
    for q in range(quarters):
        cols = slice(q * width, (q + 1) * width)
        out_ref[q, :, :width] = dot(hidden, second_ref[:, cols], ((1,), (0,))).astype(BF16)
        back = dot(pre_grad, first_ref[cols, :], ((1,), (1,))).astype(BF16)
        out_ref[q, :, width:both] = back
        total += rows_ref[q, :, :width].astype(F32) * back.astype(F32)
    total = jnp.sum(total, axis=1, keepdims=True)
    high = total.astype(BF16).astype(F32)
    extra = out_ref.shape[2] - both
    column = lax.broadcasted_iota(jnp.int32, (images, extra), 1) - 2 * place_ref[0]
    terms = jnp.where(column == 0, high, jnp.where(column == 1, total - high, 0.0)).astype(BF16)
    for q in range(quarters):
        out_ref[q, :, both:] = terms


def transposed_rows(rows, inner):
    outer = rows // inner
    to = lax.broadcasted_iota(jnp.int32, (rows, rows), 0)
    at = lax.broadcasted_iota(jnp.int32, (rows, rows), 1)
    return (at == (to % outer) * inner + to // outer).astype(BF16)


def plane_sum(rows_ref, out_ref):
    rows = out_ref.shape[0]
    order = transposed_rows(rows, 16)
    total = dot(order, rows_ref[:rows, :], ((1,), (0,)))
    total += dot(order, rows_ref[rows:, :], ((1,), (0,)))
    out_ref[...] = total.astype(BF16)


def in_order(rows_ref, out_ref):
    rows = out_ref.shape[0]
    order = transposed_rows(rows, rows // 16)
    out_ref[...] = dot(order, rows_ref[...], ((1,), (0,))).astype(BF16)


def in_order_with_totals(rows_ref, out_ref, totals_ref):
    rows, both = out_ref.shape
    order = transposed_rows(rows, rows // 16)
    out_ref[...] = dot(order, rows_ref[:, :both], ((1,), (0,))).astype(BF16)
    terms = dot(order, rows_ref[:, both:], ((1,), (0,))).astype(BF16)
    ones = jnp.ones((16, terms.shape[1]), BF16)
    totals_ref[...] = dot(ones, terms, ((1,), (1,)))[: totals_ref.shape[0]]


def tokens_back(rows_ref, totals_ref, tok_ref, up_ref, disp_ref, comb_ref, keys_ref, out_hbm, out_ref, sems):
    quarters, _, both = rows_ref.shape
    width = both // 2
    comb_grad = disp_grad = 0.0
    for q in range(quarters):
        cols = slice(q * width, (q + 1) * width)
        comb_grad += dot(up_ref[:, cols], rows_ref[q, :, :width], ((1,), (1,)))
        disp_grad += dot(tok_ref[:, cols], rows_ref[q, :, width:], ((1,), (1,)))
    comb = comb_ref[...].astype(F32)
    disp = disp_ref[...].astype(F32)
    logit = comb * (comb_grad - jnp.sum(comb * comb_grad, axis=1, keepdims=True))
    logit += disp * (disp_grad - totals_ref[:1, :])
    logit = logit.astype(BF16)
    copies = []
    for q in range(quarters):
        cols = slice(q * width, (q + 1) * width)
        part = dot(disp_ref[...], rows_ref[q, :, width:], ((1,), (0,)))
        part += dot(logit, keys_ref[cols, :], ((1,), (1,)))
        out_ref[:, cols] = part.astype(BF16)
        block = pl.ds(q * width, width)
        copy = pltpu.make_async_copy(out_ref.at[:, block], out_hbm.at[:, block], sems.at[q])
        copy.start()
        copies.append(copy)
    for copy in copies:
        copy.wait()


def vmem(count):
    return [pl.BlockSpec(memory_space=VMEM)] * count


def params(mib):
    return pltpu.CompilerParams(vmem_limit_bytes=mib * MIB)


def pick(value, at, dim=0):
    return lax.dynamic_index_in_dim(value, at, dim, keepdims=False)


TOK = ("x_lo", "core")
PLANE = ("x_lo", "y", "x_hi")
EXP = ("y", "x_hi", "z")


def chip_sum(parts, core):
    parts = parts.reshape(2, 2, *parts.shape[1:])
    arrived = lax.all_gather(pick(parts, 1 - core, 1), "core", axis=0)
    terms = (pick(parts, core, 1), pick(arrived, 1 - core))
    return sum(v.astype(F32) for v in terms).astype(BF16)


def exchanged(value):
    halves, rows, both = value.shape
    value = value.reshape(halves * rows // 16, 16, both)
    value = lax.all_to_all(value, PLANE, 0, 0, tiled=True)
    value = pl.pallas_call(
        plane_sum,
        out_shape=jax.ShapeDtypeStruct((rows, both), BF16),
        in_specs=vmem(1),
        out_specs=vmem(1)[0],
        compiler_params=params(4),
        name="plane_sum",
    )(value.reshape(halves * rows, both))
    value = value.reshape(16, rows // 16, both)
    return lax.all_to_all(value, "z", 0, 0, tiled=True).reshape(rows, both)


def body(tokens, upstream, dispatch, combine, w_in, w_out, slot_keys):
    tokens, upstream, dispatch, combine = tokens[0], upstream[0], dispatch[0], combine[0]
    rows, features = tokens.shape
    slots = dispatch.shape[1]
    quarters = 4
    width = features // quarters
    both = 2 * width
    core = lax.axis_index("core").astype(jnp.uint32)
    place = lax.axis_index(TOK).reshape(1)
    opened = pl.pallas_call(
        opening,
        out_shape=jax.ShapeDtypeStruct((8, 128), F32),
        out_specs=vmem(1)[0],
        compiler_params=params(1),
        cost_estimate=pl.CostEstimate(flops=10**10, bytes_accessed=10**7, transcendentals=0),
        name="opening",
    )()
    partial = pl.pallas_call(
        slot_sums,
        out_shape=jax.ShapeDtypeStruct((quarters, slots, both), BF16),
        in_specs=vmem(5),
        out_specs=vmem(1)[0],
        compiler_params=params(8),
        name="slot_sums",
    )(opened, dispatch, combine, tokens, upstream)
    partial, core, place = lax.optimization_barrier((partial, core, place))
    arrived = exchanged(chip_sum(partial, core))
    images = arrived.shape[0]
    arrived = pl.pallas_call(
        in_order,
        out_shape=jax.ShapeDtypeStruct((images, both), BF16),
        in_specs=vmem(1),
        out_specs=vmem(1)[0],
        compiler_params=params(4),
        name="in_order",
    )(arrived)
    arrived = lax.all_gather(arrived, TOK, axis=0)

    leaving = pl.pallas_call(
        expert,
        out_shape=jax.ShapeDtypeStruct((quarters, images, both + 128), BF16),
        in_specs=[pl.BlockSpec(memory_space=pltpu.SMEM)] + vmem(3),
        out_specs=vmem(1)[0],
        compiler_params=params(12),
        name="expert",
    )(place, arrived, w_in[0], w_out[0])
    returned = exchanged(chip_sum(leaving, core))
    returned, totals = pl.pallas_call(
        in_order_with_totals,
        out_shape=(
            jax.ShapeDtypeStruct((slots, both), BF16),
            jax.ShapeDtypeStruct((8, slots), F32),
        ),
        in_specs=vmem(1),
        out_specs=vmem(2),
        compiler_params=params(4),
        name="in_order_with_totals",
    )(returned)
    returned = lax.all_gather(returned, TOK, axis=0)

    result = pl.pallas_call(
        tokens_back,
        out_shape=jax.ShapeDtypeStruct((rows, features), BF16),
        in_specs=vmem(7),
        out_specs=pl.BlockSpec(memory_space=pl.ANY),
        scratch_shapes=[VMEM((rows, features), BF16), pltpu.SemaphoreType.DMA((quarters,))],
        compiler_params=params(12),
        name="tokens_back",
    )(returned, totals, tokens, upstream, dispatch, combine, slot_keys)
    return result[None]


def solution(mesh):
    sizes = (2, 2, 4, 2, 16)
    fine = Mesh(mesh.devices.reshape(sizes), TOK + EXP)
    placed = (
        P(EXP, TOK, None),
        P(EXP, TOK, None),
        P(EXP, TOK, None),
        P(EXP, TOK, None),
        P(EXP, None, TOK),
        P(EXP, TOK, None),
        P(),
    )
    return jax.shard_map(
        body, mesh=fine, in_specs=placed, out_specs=P(EXP, TOK, None), check_vma=False
    )
```

time: 102 us -> 101 us (level)
    all_gather x1, blocking collectives: 11.7 us -> 10.4 us  [body(): arrived = lax.all_gather(arrived, TOK, axis=0)]
where the time goes in v5:
time: 101 us
  blocking collectives  95.1 us (94%)
  Pallas kernels  4.2 us (4%)
  local copies, waits for them, and re-layouts  1.34 us (1%)
    all_to_all x2, blocking collectives, exchanged(): return lax.all_to_all(value, 'z', 0, 0, tiled=True).reshape(rows, both)  40.4 us
    all_to_all x2, blocking collectives, exchanged(): value = lax.all_to_all(value, PLANE, 0, 0, tiled=True)  22.2 us
    all_gather x1, blocking collectives, body(): returned = lax.all_gather(returned, TOK, axis=0)  11.2 us
    all_gather x2, blocking collectives, chip_sum(): arrived = lax.all_gather(pick(parts, 1 - core, 1), 'core', axis=0)  11 us
    all_gather x1, blocking collectives, body(): arrived = lax.all_gather(arrived, TOK, axis=0)  10.4 us

profile of v5, /device:TPU:1, one launch (start us, length us, event | category | flops | bytes accessed | tf_op | source)
XLA Modules:
  0.0 101.0 jit_solution(1036900432418375694)
XLA Ops:
  0.0 0.0 copy-start.6
  0.0 1.0 copy-done
  1.0 0.2 copy-done.1
  1.2 0.0 copy-done.5
  1.2 0.3 slot_sums.1
  1.6 8.7 %all-gather = bf16[4,1,128,512]{3,2,1,0:T(8,128)(2,1)S(1)} all-gather(bf16[2,1,128,512]{3,2,1,0:T(8,128)(2,1)S(1)} %get-tuple-element.18), channel_id=2, replica_groups=mesh['x_lo'=2,'core'=2,'y'=4,'x_hi'=2,'z'=16] {'core'}, dimensions={0}, use_global_device_ids=true | all-gather | bytes 786432 | tf_op jit(solution)/shard_map/all_gather | solution.py:145
  10.3 0.1 fusion.1
  10.4 0.0 copy-start.2
  10.4 0.0 copy-start.3
  10.4 10.4 %all_to_all.20 = bf16[16,16,512]{2,1,0:T(8,128)(2,1)S(1)} all-to-all(bf16[16,16,512]{2,1,0:T(8,128)(2,1)S(1)} %fusion.1), channel_id=1, replica_groups=mesh['x_lo'=2,'core'=2,'y'=4,'x_hi'=2,'z'=16] {'x_lo','y','x_hi'}, dimensions={0} | all-to-all | bytes 524288 | tf_op jit(solution)/shard_map/all_to_all | solution.py:153
  20.8 0.2 plane_sum.2
  21.0 25.4 %all_to_all.21 = bf16[16,8,512]{2,1,0:T(8,128)(2,1)S(1)} all-to-all(bf16[16,8,512]{2,1,0:T(8,128)(2,1)S(1)} %bitcast.42), channel_id=1, replica_groups=mesh['x_lo'=2,'core'=2,'y'=4,'x_hi'=2,'z'=16] {'z'}, dimensions={0} | all-to-all | bytes 262144 | tf_op jit(solution)/shard_map/all_to_all | solution.py:163
  46.4 0.2 in_order.1
  46.6 10.4 %all-gather.1 = bf16[512,512]{1,0:T(8,128)(2,1)S(1)} all-gather(bf16[128,512]{1,0:T(8,128)(2,1)S(1)} %in_order.1), channel_id=3, replica_groups=mesh['x_lo'=2,'core'=2,'y'=4,'x_hi'=2,'z'=16] {'x_lo','core'}, dimensions={0}, use_global_device_ids=true | all-gather | bytes 655360 | tf_op jit(solution)/shard_map/all_gather | solution.py:202
  57.0 1.3 %expert.1 = bf16[4,128,640]{2,1,0:T(8,128)(2,1)S(1)} custom-call(s32[1]{0:T(128)} %bitcast.4.place_ref, bf16[4,128,512]{2,1,0:T(8,128)(2,1)S(1)} %bitcast.35, bf16[1024,512]{1,0:T(8,128)(2,1)S(1)} %bitcast.37, bf16[512,1024]{1,0:T(8,128)(2,1)S(1)} %bitcast.38), custom_call_target="tpu_custom_call" | custom-call | tf_op jit(solution)/shard_map/expert/pallas_call | solution.py:204
  58.4 0.1 constant_dynamic-slice_fusion.2
  58.4 2.3 %all-gather.2 = bf16[4,1,128,640]{3,2,1,0:T(8,128)(2,1)S(1)} all-gather(bf16[2,1,128,640]{3,2,1,0:T(8,128)(2,1)S(1)} %get-tuple-element.16), channel_id=4, replica_groups=mesh['x_lo'=2,'core'=2,'y'=4,'x_hi'=2,'z'=16] {'core'}, dimensions={0}, use_global_device_ids=true | all-gather | bytes 983040 | tf_op jit(solution)/shard_map/all_gather | solution.py:145
  60.7 0.1 fusion
  60.8 11.8 %all_to_all.22 = bf16[16,16,640]{2,1,0:T(8,128)(2,1)S(1)} all-to-all(bf16[16,16,640]{2,1,0:T(8,128)(2,1)S(1)} %fusion), channel_id=1, replica_groups=mesh['x_lo'=2,'core'=2,'y'=4,'x_hi'=2,'z'=16] {'x_lo','y','x_hi'}, dimensions={0} | all-to-all | bytes 655360 | tf_op jit(solution)/shard_map/all_to_all | solution.py:153
  72.6 0.2 plane_sum.3
  72.8 15.1 %all_to_all.23 = bf16[16,8,640]{2,1,0:T(8,128)(2,1)S(1)} all-to-all(bf16[16,8,640]{2,1,0:T(8,128)(2,1)S(1)} %bitcast.41), channel_id=1, replica_groups=mesh['x_lo'=2,'core'=2,'y'=4,'x_hi'=2,'z'=16] {'z'}, dimensions={0} | all-to-all | bytes 327680 | tf_op jit(solution)/shard_map/all_to_all | solution.py:163
  87.9 0.3 in_order_with_totals.1
  88.2 11.2 %all-gather.3 = bf16[512,512]{1,0:T(8,128)(2,1)S(1)} all-gather(bf16[128,512]{1,0:T(8,128)(2,1)S(1)} %get-tuple-element.13), channel_id=5, replica_groups=mesh['x_lo'=2,'core'=2,'y'=4,'x_hi'=2,'z'=16] {'x_lo','core'}, dimensions={0}, use_global_device_ids=true | all-gather | bytes 655360 | tf_op jit(solution)/shard_map/all_gather | solution.py:224
  99.4 1.6 %tokens_back.1 = bf16[256,1024]{1,0:T(8,128)(2,1)} custom-call(bf16[4,128,512]{2,1,0:T(8,128)(2,1)S(1)} %bitcast.29, f32[8,128]{1,0:T(8,128)S(1)} %get-tuple-element.14.totals_ref, bf16[256,1024]{1,0:T(8,128)(2,1)S(1)} %bitcast.31, bf16[256,1024]{1,0:T(8,128)(2,1)S(1)} %bitcast.33, bf16[256,128]{1,0:T(8,128)(2,1)S(1)} %bitcast.45, ...), custom_call_target="tpu_custom_call" | custom-call | tf_op jit(solution)/shard_map/tokens_back/pallas_call | solution.py:226
  (12 shorter events, 0.1 us)
Async XLA Ops:
  0.0 1.0 %copy-start = (bf16[1,256,1024]{2,1,0:T(8,128)(2,1)S(1)}, bf16[1,256,1024]{2,1,0:T(8,128)(2,1)}, u32[]{:S(2)}) copy-start(bf16[1,256,1024]{2,1,0:T(8,128)(2,1)} %param.7) | copy-start | bytes 1572868
  0.0 1.2 %copy-start.1 = (bf16[1,256,1024]{2,1,0:T(8,128)(2,1)S(1)}, bf16[1,256,1024]{2,1,0:T(8,128)(2,1)}, u32[]{:S(2)}) copy-start(bf16[1,256,1024]{2,1,0:T(8,128)(2,1)} %param.8) | copy-start | bytes 1572868
  0.0 1.2 %copy-start.5 = (bf16[1,256,128]{2,1,0:T(8,128)(2,1)S(1)}, bf16[1,256,128]{2,1,0:T(8,128)(2,1)}, u32[]{:S(2)}) copy-start(bf16[1,256,128]{2,1,0:T(8,128)(2,1)} %param.9) | copy-start | bytes 196612
  0.0 1.2 %copy-start.6 = (bf16[1,256,128]{2,1,0:T(8,128)(2,1)S(1)}, bf16[1,256,128]{2,1,0:T(8,128)(2,1)}, u32[]{:S(2)}) copy-start(bf16[1,256,128]{2,1,0:T(8,128)(2,1)} %param.10) | copy-start | bytes 196612
  10.4 46.6 %copy-start.2 = (bf16[1,1024,512]{2,1,0:T(8,128)(2,1)S(1)}, bf16[1,1024,512]{2,1,0:T(8,128)(2,1)}, u32[]{:S(2)}) copy-start(bf16[1,1024,512]{2,1,0:T(8,128)(2,1)} %param.11) | copy-start | bytes 3145732
  10.4 46.6 %copy-start.3 = (bf16[1,512,1024]{2,1,0:T(8,128)(2,1)S(1)}, bf16[1,512,1024]{2,1,0:T(8,128)(2,1)}, u32[]{:S(2)}) copy-start(bf16[1,512,1024]{2,1,0:T(8,128)(2,1)} %param.12) | copy-start | bytes 3145732
  88.2 11.2 %copy-start.4 = (bf16[1024,128]{1,0:T(8,128)(2,1)S(1)}, bf16[1024,128]{1,0:T(8,128)(2,1)}, u32[]{:S(2)}) copy-start(bf16[1024,128]{1,0:T(8,128)(2,1)} %keys_ref.1) | copy-start | bytes 786436

commit v6 on v4

--- a/solution.py
+++ b/solution.py
@@ -43,11 +43,12 @@
 def expert(rows_ref, first_ref, second_ref, out_ref):
     quarters, _, both = rows_ref.shape
     width = both // 2
-    pre_act = hidden_grad = 0.0
-    for q in range(quarters):
-        cols = slice(q * width, (q + 1) * width)
-        pre_act += dot(rows_ref[q, :, :width], first_ref[cols, :], ((1,), (0,)))
-        hidden_grad += dot(rows_ref[q, :, width:], second_ref[:, cols], ((1,), (1,)))
+    inputs, grads = (
+        jnp.concatenate([rows_ref[q, :, at : at + width] for q in range(quarters)], axis=1)
+        for at in (0, width)
+    )
+    pre_act = dot(inputs, first_ref[...], ((1,), (0,)))
+    hidden_grad = dot(grads, second_ref[...], ((1,), (1,)))
     value, slope = gelu_parts(pre_act)
     hidden = value.astype(BF16)
     pre_grad = (hidden_grad * slope).astype(BF16)

time: 101 us -> 101 us (level)
  no operation moved by 1% of the time
where the time goes in v6:
time: 101 us
  blocking collectives  95.5 us (95%)
  Pallas kernels  3.58 us (4%)
  local copies, waits for them, and re-layouts  1.31 us (1%)
    all_to_all x1, blocking collectives, exchanged(): lax.all_to_all(blocks, EXP, split_axis=0, concat_axis=0, tiled=True)  33.6 us
    all_to_all x1, blocking collectives, body(): lax.all_to_all(leaving, 'z', 0, 0, tiled=True).reshape(slots, both)  14.6 us
    all_gather x2, blocking collectives, core_terms(): arrived = lax.all_gather(given, 'core', axis=0)  10.9 us
    all_to_all x1, blocking collectives, body(): lax.all_to_all(leaving.reshape(16, 16, both), plane, 0, 0, tiled=True)  10.5 us
    all_gather x1, blocking collectives, body(): returned = lax.all_gather(returned, TOK, axis=0)  10.4 us
    all_gather x1, blocking collectives, body(): arrived = lax.all_gather(arrived, TOK, axis=0)  9.93 us
    all_gather x1, blocking collectives, tok_sum(): across = lax.all_gather(half(1 - xl).astype(BF16), 'x_lo', axis=0)  5.52 us

profile of v6, /device:TPU:1, one launch (start us, length us, event | category | flops | bytes accessed | tf_op | source)
XLA Modules:
  0.0 100.7 jit_solution(135734010548153883)
XLA Ops:
  0.0 0.0 copy-start.6
  0.1 1.0 copy-done
  1.0 0.2 copy-done.1
  1.2 0.0 copy-done.5
  1.2 0.0 copy-done.6
  1.2 0.3 slot_sums.1
  1.6 8.7 %all-gather = bf16[4,1,128,512]{3,2,1,0:T(8,128)(2,1)S(1)} all-gather(bf16[2,1,128,512]{3,2,1,0:T(8,128)(2,1)S(1)} %constant_dynamic-slice_fusion.2), channel_id=2, replica_groups=mesh['x_lo'=2,'core'=2,'y'=4,'x_hi'=2,'z'=16] {'core'}, dimensions={0}, use_global_device_ids=true | all-gather | bytes 786432 | tf_op jit(solution)/shard_map/all_gather | solution.py:137
  10.3 0.0 copy-start.3
  10.3 5.5 %all-gather.1 = bf16[2,1,128,512]{3,2,1,0:T(8,128)(2,1)S(1)} all-gather(bf16[1,1,128,512]{3,2,1,0:T(8,128)(2,1)S(1)} %add_convert_fusion.1), channel_id=3, replica_groups=mesh['x_lo'=2,'core'=2,'y'=4,'x_hi'=2,'z'=16] {'x_lo'}, dimensions={0}, use_global_device_ids=true | all-gather | bytes 393216 | tf_op jit(solution)/shard_map/all_gather | solution.py:147
  15.8 0.1 add_convert_fusion
  15.9 33.6 %all_to_all.15 = bf16[128,4,128]{2,1,0:T(4,128)(2,1)S(1)} all-to-all(bf16[128,4,128]{2,1,0:T(4,128)(2,1)S(1)} %reshape.100), channel_id=1, replica_groups=mesh['x_lo'=2,'core'=2,'y'=4,'x_hi'=2,'z'=16] {'y','x_hi','z'}, dimensions={0} | all-to-all | bytes 262144 | tf_op jit(solution)/shard_map/all_to_all | solution.py:158
  49.6 9.9 %all-gather.2 = bf16[512,512]{1,0:T(8,128)(2,1)S(1)} all-gather(bf16[128,512]{1,0:T(8,128)(2,1)S(1)} %bitcast.52), channel_id=4, replica_groups=mesh['x_lo'=2,'core'=2,'y'=4,'x_hi'=2,'z'=16] {'x_lo','core'}, dimensions={0}, use_global_device_ids=true | all-gather | bytes 655360 | tf_op jit(solution)/shard_map/all_gather | solution.py:191
  59.5 0.0 copy-done.3
  59.5 0.0 copy-done.2
  59.5 1.1 %expert.1 = bf16[4,128,512]{2,1,0:T(8,128)(2,1)S(1)} custom-call(bf16[4,128,512]{2,1,0:T(8,128)(2,1)S(1)} %bitcast.36, bf16[1024,512]{1,0:T(8,128)(2,1)S(1)} %bitcast.38, bf16[512,1024]{1,0:T(8,128)(2,1)S(1)} %bitcast.39), custom_call_target="tpu_custom_call" | custom-call | tf_op jit(solution)/shard_map/expert/pallas_call | solution.py:193
  60.7 2.2 %all-gather.3 = bf16[4,1,128,512]{3,2,1,0:T(8,128)(2,1)S(1)} all-gather(bf16[2,1,128,512]{3,2,1,0:T(8,128)(2,1)S(1)} %get-tuple-element.12), channel_id=5, replica_groups=mesh['x_lo'=2,'core'=2,'y'=4,'x_hi'=2,'z'=16] {'core'}, dimensions={0}, use_global_device_ids=true | all-gather | bytes 786432 | tf_op jit(solution)/shard_map/all_gather | solution.py:137
  62.9 0.1 fusion
  63.0 10.5 %all_to_all.16 = bf16[16,16,512]{2,1,0:T(8,128)(2,1)S(1)} all-to-all(bf16[16,16,512]{2,1,0:T(8,128)(2,1)S(1)} %fusion), channel_id=1, replica_groups=mesh['x_lo'=2,'core'=2,'y'=4,'x_hi'=2,'z'=16] {'x_lo','y','x_hi'}, dimensions={0} | all-to-all | bytes 524288 | tf_op jit(solution)/shard_map/all_to_all | solution.py:204
  73.5 0.2 plane_sum.1
  73.7 14.6 %all_to_all.17 = bf16[16,8,512]{2,1,0:T(8,128)(2,1)S(1)} all-to-all(bf16[16,8,512]{2,1,0:T(8,128)(2,1)S(1)} %bitcast.42), channel_id=1, replica_groups=mesh['x_lo'=2,'core'=2,'y'=4,'x_hi'=2,'z'=16] {'z'}, dimensions={0} | all-to-all | bytes 262144 | tf_op jit(solution)/shard_map/all_to_all | solution.py:214
  88.4 0.3 with_totals.1
  88.7 10.4 %all-gather.4 = bf16[576,512]{1,0:T(8,128)(2,1)S(1)} all-gather(bf16[144,512]{1,0:T(8,128)(2,1)S(1)} %with_totals.1), channel_id=6, replica_groups=mesh['x_lo'=2,'core'=2,'y'=4,'x_hi'=2,'z'=16] {'x_lo','core'}, dimensions={0}, use_global_device_ids=true | all-gather | bytes 737280 | tf_op jit(solution)/shard_map/all_gather | solution.py:223
  99.0 0.0 copy-done.4
  99.0 1.6 %tokens_back.1 = bf16[256,1024]{1,0:T(8,128)(2,1)} custom-call(bf16[4,144,512]{2,1,0:T(8,128)(2,1)S(1)} %bitcast.27, bf16[256,1024]{1,0:T(8,128)(2,1)S(1)} %bitcast.29, bf16[256,1024]{1,0:T(8,128)(2,1)S(1)} %bitcast.31, bf16[256,128]{1,0:T(8,128)(2,1)S(1)} %bitcast.44, bf16[256,128]{1,0:T(8,128)(2,1)S(1)} %bitcast.46, bf16[1024,128]{1,0:T(8,128)(2,1)S(1)} %copy-done.4), custom_call_target="tpu_custom_call" | custom-call | tf_op jit(solution)/shard_map/tokens_back/pallas_call | solution.py:225
  (12 shorter events, 0.2 us)
Async XLA Ops:
  0.0 1.0 %copy-start = (bf16[1,256,1024]{2,1,0:T(8,128)(2,1)S(1)}, bf16[1,256,1024]{2,1,0:T(8,128)(2,1)}, u32[]{:S(2)}) copy-start(bf16[1,256,1024]{2,1,0:T(8,128)(2,1)} %param.7) | copy-start | bytes 1572868
  0.0 1.2 %copy-start.1 = (bf16[1,256,1024]{2,1,0:T(8,128)(2,1)S(1)}, bf16[1,256,1024]{2,1,0:T(8,128)(2,1)}, u32[]{:S(2)}) copy-start(bf16[1,256,1024]{2,1,0:T(8,128)(2,1)} %param.8) | copy-start | bytes 1572868
  0.0 1.2 %copy-start.5 = (bf16[1,256,128]{2,1,0:T(8,128)(2,1)S(1)}, bf16[1,256,128]{2,1,0:T(8,128)(2,1)}, u32[]{:S(2)}) copy-start(bf16[1,256,128]{2,1,0:T(8,128)(2,1)} %param.9) | copy-start | bytes 196612
  0.0 1.2 %copy-start.6 = (bf16[1,256,128]{2,1,0:T(8,128)(2,1)S(1)}, bf16[1,256,128]{2,1,0:T(8,128)(2,1)}, u32[]{:S(2)}) copy-start(bf16[1,256,128]{2,1,0:T(8,128)(2,1)} %param.10) | copy-start | bytes 196612
  10.3 49.2 %copy-start.3 = (bf16[1,512,1024]{2,1,0:T(8,128)(2,1)S(1)}, bf16[1,512,1024]{2,1,0:T(8,128)(2,1)}, u32[]{:S(2)}) copy-start(bf16[1,512,1024]{2,1,0:T(8,128)(2,1)} %param.12) | copy-start | bytes 3145732
  15.8 43.7 %copy-start.2 = (bf16[1,1024,512]{2,1,0:T(8,128)(2,1)S(1)}, bf16[1,1024,512]{2,1,0:T(8,128)(2,1)}, u32[]{:S(2)}) copy-start(bf16[1,1024,512]{2,1,0:T(8,128)(2,1)} %param.11) | copy-start | bytes 3145732
  88.7 10.4 %copy-start.4 = (bf16[1024,128]{1,0:T(8,128)(2,1)S(1)}, bf16[1024,128]{1,0:T(8,128)(2,1)}, u32[]{:S(2)}) copy-start(bf16[1024,128]{1,0:T(8,128)(2,1)} %keys_ref.1) | copy-start | bytes 786436

commit v7 on v6

--- a/solution.py
+++ b/solution.py
@@ -67,10 +67,11 @@
 
 def plane_sum(rows_ref, out_ref):
     rows = out_ref.shape[0]
-    order = transposed_rows(rows, 16)
-    total = dot(order, rows_ref[:rows, :], ((1,), (0,)))
-    total += dot(order, rows_ref[rows:, :], ((1,), (0,)))
-    out_ref[...] = total.astype(BF16)
+    to = lax.broadcasted_iota(jnp.int32, (rows, 2 * rows), 0)
+    at = lax.broadcasted_iota(jnp.int32, (rows, 2 * rows), 1)
+    plane, z = at // 16 % 8, at % 16
+    order = (to == z * 8 + plane).astype(BF16)
+    out_ref[...] = dot(order, rows_ref[...], ((1,), (0,))).astype(BF16)
 
 
 def with_totals(back_ref, slots_ref, out_ref):
@@ -80,9 +81,10 @@
     back = dot(order, back_ref[...], ((1,), (0,)))
     out_ref[:rows, :] = back.astype(BF16)
     product = slots_ref[:, :width].astype(F32) * back[:, width:]
+    product = product[:, : width // 2] + product[:, width // 2 :]
     high = product.astype(BF16)
     low = (product - high.astype(F32)).astype(BF16)
-    ones = jnp.ones((16, width), BF16)
+    ones = jnp.ones((16, width // 2), BF16)
     total = dot(ones, high, ((1,), (1,))) + dot(ones, low, ((1,), (1,)))
     total_high = total.astype(BF16)
     out_ref[rows:, :rows] = total_high

time: 101 us -> 101 us (level)
  no operation moved by 1% of the time
where the time goes in v7:
time: 101 us
  blocking collectives  95.5 us (95%)
  Pallas kernels  3.55 us (4%)
  local copies, waits for them, and re-layouts  1.31 us (1%)
    all_to_all x1, blocking collectives, exchanged(): lax.all_to_all(blocks, EXP, split_axis=0, concat_axis=0, tiled=True)  33.6 us
    all_to_all x1, blocking collectives, body(): lax.all_to_all(leaving, 'z', 0, 0, tiled=True).reshape(slots, both)  14.6 us
    all_gather x2, blocking collectives, core_terms(): arrived = lax.all_gather(given, 'core', axis=0)  10.9 us
    all_to_all x1, blocking collectives, body(): lax.all_to_all(leaving.reshape(16, 16, both), plane, 0, 0, tiled=True)  10.5 us
    all_gather x1, blocking collectives, body(): returned = lax.all_gather(returned, TOK, axis=0)  10.4 us
    all_gather x1, blocking collectives, body(): arrived = lax.all_gather(arrived, TOK, axis=0)  9.93 us
    all_gather x1, blocking collectives, tok_sum(): across = lax.all_gather(half(1 - xl).astype(BF16), 'x_lo', axis=0)  5.52 us

profile of v7, /device:TPU:1, one launch (start us, length us, event | category | flops | bytes accessed | tf_op | source)
XLA Modules:
  0.0 100.6 jit_solution(12862455754980057256)
XLA Ops:
  0.0 0.0 copy-start.6
  0.1 1.0 copy-done
  1.0 0.2 copy-done.1
  1.2 0.0 copy-done.5
  1.2 0.0 copy-done.6
  1.2 0.3 slot_sums.1
  1.6 8.7 %all-gather = bf16[4,1,128,512]{3,2,1,0:T(8,128)(2,1)S(1)} all-gather(bf16[2,1,128,512]{3,2,1,0:T(8,128)(2,1)S(1)} %constant_dynamic-slice_fusion.2), channel_id=2, replica_groups=mesh['x_lo'=2,'core'=2,'y'=4,'x_hi'=2,'z'=16] {'core'}, dimensions={0}, use_global_device_ids=true | all-gather | bytes 786432 | tf_op jit(solution)/shard_map/all_gather | solution.py:139
  10.3 0.0 copy-start.3
  10.3 5.5 %all-gather.1 = bf16[2,1,128,512]{3,2,1,0:T(8,128)(2,1)S(1)} all-gather(bf16[1,1,128,512]{3,2,1,0:T(8,128)(2,1)S(1)} %add_convert_fusion.1), channel_id=3, replica_groups=mesh['x_lo'=2,'core'=2,'y'=4,'x_hi'=2,'z'=16] {'x_lo'}, dimensions={0}, use_global_device_ids=true | all-gather | bytes 393216 | tf_op jit(solution)/shard_map/all_gather | solution.py:149
  15.8 0.1 add_convert_fusion
  15.9 33.6 %all_to_all.15 = bf16[128,4,128]{2,1,0:T(4,128)(2,1)S(1)} all-to-all(bf16[128,4,128]{2,1,0:T(4,128)(2,1)S(1)} %reshape.100), channel_id=1, replica_groups=mesh['x_lo'=2,'core'=2,'y'=4,'x_hi'=2,'z'=16] {'y','x_hi','z'}, dimensions={0} | all-to-all | bytes 262144 | tf_op jit(solution)/shard_map/all_to_all | solution.py:160
  49.6 9.9 %all-gather.2 = bf16[512,512]{1,0:T(8,128)(2,1)S(1)} all-gather(bf16[128,512]{1,0:T(8,128)(2,1)S(1)} %bitcast.52), channel_id=4, replica_groups=mesh['x_lo'=2,'core'=2,'y'=4,'x_hi'=2,'z'=16] {'x_lo','core'}, dimensions={0}, use_global_device_ids=true | all-gather | bytes 655360 | tf_op jit(solution)/shard_map/all_gather | solution.py:193
  59.5 0.0 copy-done.3
  59.5 0.0 copy-done.2
  59.5 1.1 %expert.1 = bf16[4,128,512]{2,1,0:T(8,128)(2,1)S(1)} custom-call(bf16[4,128,512]{2,1,0:T(8,128)(2,1)S(1)} %bitcast.36, bf16[1024,512]{1,0:T(8,128)(2,1)S(1)} %bitcast.38, bf16[512,1024]{1,0:T(8,128)(2,1)S(1)} %bitcast.39), custom_call_target="tpu_custom_call" | custom-call | tf_op jit(solution)/shard_map/expert/pallas_call | solution.py:195
  60.7 2.2 %all-gather.3 = bf16[4,1,128,512]{3,2,1,0:T(8,128)(2,1)S(1)} all-gather(bf16[2,1,128,512]{3,2,1,0:T(8,128)(2,1)S(1)} %get-tuple-element.12), channel_id=5, replica_groups=mesh['x_lo'=2,'core'=2,'y'=4,'x_hi'=2,'z'=16] {'core'}, dimensions={0}, use_global_device_ids=true | all-gather | bytes 786432 | tf_op jit(solution)/shard_map/all_gather | solution.py:139
  62.9 0.1 fusion
  63.0 10.5 %all_to_all.16 = bf16[16,16,512]{2,1,0:T(8,128)(2,1)S(1)} all-to-all(bf16[16,16,512]{2,1,0:T(8,128)(2,1)S(1)} %fusion), channel_id=1, replica_groups=mesh['x_lo'=2,'core'=2,'y'=4,'x_hi'=2,'z'=16] {'x_lo','y','x_hi'}, dimensions={0} | all-to-all | bytes 524288 | tf_op jit(solution)/shard_map/all_to_all | solution.py:206
  73.5 0.2 plane_sum.1
  73.7 14.6 %all_to_all.17 = bf16[16,8,512]{2,1,0:T(8,128)(2,1)S(1)} all-to-all(bf16[16,8,512]{2,1,0:T(8,128)(2,1)S(1)} %bitcast.42), channel_id=1, replica_groups=mesh['x_lo'=2,'core'=2,'y'=4,'x_hi'=2,'z'=16] {'z'}, dimensions={0} | all-to-all | bytes 262144 | tf_op jit(solution)/shard_map/all_to_all | solution.py:216
  88.3 0.3 with_totals.1
  88.6 10.4 %all-gather.4 = bf16[576,512]{1,0:T(8,128)(2,1)S(1)} all-gather(bf16[144,512]{1,0:T(8,128)(2,1)S(1)} %with_totals.1), channel_id=6, replica_groups=mesh['x_lo'=2,'core'=2,'y'=4,'x_hi'=2,'z'=16] {'x_lo','core'}, dimensions={0}, use_global_device_ids=true | all-gather | bytes 737280 | tf_op jit(solution)/shard_map/all_gather | solution.py:225
  99.0 0.0 copy-done.4
  99.0 1.6 %tokens_back.1 = bf16[256,1024]{1,0:T(8,128)(2,1)} custom-call(bf16[4,144,512]{2,1,0:T(8,128)(2,1)S(1)} %bitcast.27, bf16[256,1024]{1,0:T(8,128)(2,1)S(1)} %bitcast.29, bf16[256,1024]{1,0:T(8,128)(2,1)S(1)} %bitcast.31, bf16[256,128]{1,0:T(8,128)(2,1)S(1)} %bitcast.44, bf16[256,128]{1,0:T(8,128)(2,1)S(1)} %bitcast.46, bf16[1024,128]{1,0:T(8,128)(2,1)S(1)} %copy-done.4), custom_call_target="tpu_custom_call" | custom-call | tf_op jit(solution)/shard_map/tokens_back/pallas_call | solution.py:227
  (12 shorter events, 0.2 us)
Async XLA Ops:
  0.0 1.0 %copy-start = (bf16[1,256,1024]{2,1,0:T(8,128)(2,1)S(1)}, bf16[1,256,1024]{2,1,0:T(8,128)(2,1)}, u32[]{:S(2)}) copy-start(bf16[1,256,1024]{2,1,0:T(8,128)(2,1)} %param.7) | copy-start | bytes 1572868
  0.0 1.2 %copy-start.1 = (bf16[1,256,1024]{2,1,0:T(8,128)(2,1)S(1)}, bf16[1,256,1024]{2,1,0:T(8,128)(2,1)}, u32[]{:S(2)}) copy-start(bf16[1,256,1024]{2,1,0:T(8,128)(2,1)} %param.8) | copy-start | bytes 1572868
  0.0 1.2 %copy-start.5 = (bf16[1,256,128]{2,1,0:T(8,128)(2,1)S(1)}, bf16[1,256,128]{2,1,0:T(8,128)(2,1)}, u32[]{:S(2)}) copy-start(bf16[1,256,128]{2,1,0:T(8,128)(2,1)} %param.9) | copy-start | bytes 196612
  0.0 1.2 %copy-start.6 = (bf16[1,256,128]{2,1,0:T(8,128)(2,1)S(1)}, bf16[1,256,128]{2,1,0:T(8,128)(2,1)}, u32[]{:S(2)}) copy-start(bf16[1,256,128]{2,1,0:T(8,128)(2,1)} %param.10) | copy-start | bytes 196612
  10.3 49.2 %copy-start.3 = (bf16[1,512,1024]{2,1,0:T(8,128)(2,1)S(1)}, bf16[1,512,1024]{2,1,0:T(8,128)(2,1)}, u32[]{:S(2)}) copy-start(bf16[1,512,1024]{2,1,0:T(8,128)(2,1)} %param.12) | copy-start | bytes 3145732
  15.8 43.7 %copy-start.2 = (bf16[1,1024,512]{2,1,0:T(8,128)(2,1)S(1)}, bf16[1,1024,512]{2,1,0:T(8,128)(2,1)}, u32[]{:S(2)}) copy-start(bf16[1,1024,512]{2,1,0:T(8,128)(2,1)} %param.11) | copy-start | bytes 3145732
  88.6 10.4 %copy-start.4 = (bf16[1024,128]{1,0:T(8,128)(2,1)S(1)}, bf16[1024,128]{1,0:T(8,128)(2,1)}, u32[]{:S(2)}) copy-start(bf16[1024,128]{1,0:T(8,128)(2,1)} %keys_ref.1) | copy-start | bytes 786436

commit v8 on v7

--- a/solution.py
+++ b/solution.py
@@ -167,7 +167,7 @@
     quarters = 4
     width = features // quarters
     both = 2 * width
-    xl, core = lax.axis_index("x_lo"), lax.axis_index("core")
+    xl, core = (lax.axis_index(axis).astype(jnp.uint32) for axis in TOK)
     parts = jax.ShapeDtypeStruct((quarters, slots, both), BF16)
 
     opened = pl.pallas_call(

time: 101 us -> 101 us (level)
  no operation moved by 1% of the time
where the time goes in v8:
time: 101 us
  blocking collectives  95.5 us (95%)
  Pallas kernels  3.55 us (4%)
  local copies, waits for them, and re-layouts  1.34 us (1%)
    all_to_all x1, blocking collectives, exchanged(): lax.all_to_all(blocks, EXP, split_axis=0, concat_axis=0, tiled=True)  33.6 us
    all_to_all x1, blocking collectives, body(): lax.all_to_all(leaving, 'z', 0, 0, tiled=True).reshape(slots, both)  14.6 us
    all_gather x2, blocking collectives, core_terms(): arrived = lax.all_gather(given, 'core', axis=0)  10.9 us
    all_to_all x1, blocking collectives, body(): lax.all_to_all(leaving.reshape(16, 16, both), plane, 0, 0, tiled=True)  10.5 us
    all_gather x1, blocking collectives, body(): returned = lax.all_gather(returned, TOK, axis=0)  10.4 us
    all_gather x1, blocking collectives, body(): arrived = lax.all_gather(arrived, TOK, axis=0)  9.93 us
    all_gather x1, blocking collectives, tok_sum(): across = lax.all_gather(half(1 - xl).astype(BF16), 'x_lo', axis=0)  5.52 us

profile of v8, /device:TPU:1, one launch (start us, length us, event | category | flops | bytes accessed | tf_op | source)
XLA Modules:
  0.0 100.6 jit_solution(11052728688265479264)
XLA Ops:
  0.0 0.0 copy-start.6
  0.0 1.0 %copy-done = bf16[1,256,1024]{2,1,0:T(8,128)(2,1)S(1)} copy-done((bf16[1,256,1024]{2,1,0:T(8,128)(2,1)S(1)}, bf16[1,256,1024]{2,1,0:T(8,128)(2,1)}, u32[]{:S(2)}) %copy-start) | copy-done | bytes 524312
  1.0 0.2 copy-done.1
  1.2 0.0 copy-done.5
  1.2 0.0 copy-done.6
  1.2 0.3 slot_sums.1
  1.6 8.7 %all-gather = bf16[4,1,128,512]{3,2,1,0:T(8,128)(2,1)S(1)} all-gather(bf16[2,1,128,512]{3,2,1,0:T(8,128)(2,1)S(1)} %constant_dynamic-slice_fusion.2), channel_id=2, replica_groups=mesh['x_lo'=2,'core'=2,'y'=4,'x_hi'=2,'z'=16] {'core'}, dimensions={0}, use_global_device_ids=true | all-gather | bytes 786432 | tf_op jit(solution)/shard_map/all_gather | solution.py:139
  10.3 0.0 copy-start.3
  10.3 5.5 %all-gather.1 = bf16[2,1,128,512]{3,2,1,0:T(8,128)(2,1)S(1)} all-gather(bf16[1,1,128,512]{3,2,1,0:T(8,128)(2,1)S(1)} %add_convert_fusion.1), channel_id=3, replica_groups=mesh['x_lo'=2,'core'=2,'y'=4,'x_hi'=2,'z'=16] {'x_lo'}, dimensions={0}, use_global_device_ids=true | all-gather | bytes 393216 | tf_op jit(solution)/shard_map/all_gather | solution.py:149
  15.8 0.1 add_convert_fusion
  15.9 33.6 %all_to_all.15 = bf16[128,4,128]{2,1,0:T(4,128)(2,1)S(1)} all-to-all(bf16[128,4,128]{2,1,0:T(4,128)(2,1)S(1)} %reshape.100), channel_id=1, replica_groups=mesh['x_lo'=2,'core'=2,'y'=4,'x_hi'=2,'z'=16] {'y','x_hi','z'}, dimensions={0} | all-to-all | bytes 262144 | tf_op jit(solution)/shard_map/all_to_all | solution.py:160
  49.6 9.9 %all-gather.2 = bf16[512,512]{1,0:T(8,128)(2,1)S(1)} all-gather(bf16[128,512]{1,0:T(8,128)(2,1)S(1)} %bitcast.52), channel_id=4, replica_groups=mesh['x_lo'=2,'core'=2,'y'=4,'x_hi'=2,'z'=16] {'x_lo','core'}, dimensions={0}, use_global_device_ids=true | all-gather | bytes 655360 | tf_op jit(solution)/shard_map/all_gather | solution.py:193
  59.5 0.0 copy-done.3
  59.5 0.0 copy-done.2
  59.5 1.1 %expert.1 = bf16[4,128,512]{2,1,0:T(8,128)(2,1)S(1)} custom-call(bf16[4,128,512]{2,1,0:T(8,128)(2,1)S(1)} %bitcast.36, bf16[1024,512]{1,0:T(8,128)(2,1)S(1)} %bitcast.38, bf16[512,1024]{1,0:T(8,128)(2,1)S(1)} %bitcast.39), custom_call_target="tpu_custom_call" | custom-call | tf_op jit(solution)/shard_map/expert/pallas_call | solution.py:195
  60.7 2.2 %all-gather.3 = bf16[4,1,128,512]{3,2,1,0:T(8,128)(2,1)S(1)} all-gather(bf16[2,1,128,512]{3,2,1,0:T(8,128)(2,1)S(1)} %get-tuple-element.12), channel_id=5, replica_groups=mesh['x_lo'=2,'core'=2,'y'=4,'x_hi'=2,'z'=16] {'core'}, dimensions={0}, use_global_device_ids=true | all-gather | bytes 786432 | tf_op jit(solution)/shard_map/all_gather | solution.py:139
  62.9 0.1 fusion
  63.0 10.5 %all_to_all.16 = bf16[16,16,512]{2,1,0:T(8,128)(2,1)S(1)} all-to-all(bf16[16,16,512]{2,1,0:T(8,128)(2,1)S(1)} %fusion), channel_id=1, replica_groups=mesh['x_lo'=2,'core'=2,'y'=4,'x_hi'=2,'z'=16] {'x_lo','y','x_hi'}, dimensions={0} | all-to-all | bytes 524288 | tf_op jit(solution)/shard_map/all_to_all | solution.py:206
  73.5 0.2 plane_sum.1
  73.7 14.6 %all_to_all.17 = bf16[16,8,512]{2,1,0:T(8,128)(2,1)S(1)} all-to-all(bf16[16,8,512]{2,1,0:T(8,128)(2,1)S(1)} %bitcast.42), channel_id=1, replica_groups=mesh['x_lo'=2,'core'=2,'y'=4,'x_hi'=2,'z'=16] {'z'}, dimensions={0} | all-to-all | bytes 262144 | tf_op jit(solution)/shard_map/all_to_all | solution.py:216
  88.3 0.3 with_totals.1
  88.6 10.4 %all-gather.4 = bf16[576,512]{1,0:T(8,128)(2,1)S(1)} all-gather(bf16[144,512]{1,0:T(8,128)(2,1)S(1)} %with_totals.1), channel_id=6, replica_groups=mesh['x_lo'=2,'core'=2,'y'=4,'x_hi'=2,'z'=16] {'x_lo','core'}, dimensions={0}, use_global_device_ids=true | all-gather | bytes 737280 | tf_op jit(solution)/shard_map/all_gather | solution.py:225
  99.0 0.0 copy-done.4
  99.0 1.6 %tokens_back.1 = bf16[256,1024]{1,0:T(8,128)(2,1)} custom-call(bf16[4,144,512]{2,1,0:T(8,128)(2,1)S(1)} %bitcast.27, bf16[256,1024]{1,0:T(8,128)(2,1)S(1)} %bitcast.29, bf16[256,1024]{1,0:T(8,128)(2,1)S(1)} %bitcast.31, bf16[256,128]{1,0:T(8,128)(2,1)S(1)} %bitcast.44, bf16[256,128]{1,0:T(8,128)(2,1)S(1)} %bitcast.46, bf16[1024,128]{1,0:T(8,128)(2,1)S(1)} %copy-done.4), custom_call_target="tpu_custom_call" | custom-call | tf_op jit(solution)/shard_map/tokens_back/pallas_call | solution.py:227
  (12 shorter events, 0.2 us)
Async XLA Ops:
  0.0 1.0 %copy-start = (bf16[1,256,1024]{2,1,0:T(8,128)(2,1)S(1)}, bf16[1,256,1024]{2,1,0:T(8,128)(2,1)}, u32[]{:S(2)}) copy-start(bf16[1,256,1024]{2,1,0:T(8,128)(2,1)} %param.7) | copy-start | bytes 1572868
  0.0 1.2 %copy-start.1 = (bf16[1,256,1024]{2,1,0:T(8,128)(2,1)S(1)}, bf16[1,256,1024]{2,1,0:T(8,128)(2,1)}, u32[]{:S(2)}) copy-start(bf16[1,256,1024]{2,1,0:T(8,128)(2,1)} %param.8) | copy-start | bytes 1572868
  0.0 1.2 %copy-start.5 = (bf16[1,256,128]{2,1,0:T(8,128)(2,1)S(1)}, bf16[1,256,128]{2,1,0:T(8,128)(2,1)}, u32[]{:S(2)}) copy-start(bf16[1,256,128]{2,1,0:T(8,128)(2,1)} %param.9) | copy-start | bytes 196612
  0.0 1.2 %copy-start.6 = (bf16[1,256,128]{2,1,0:T(8,128)(2,1)S(1)}, bf16[1,256,128]{2,1,0:T(8,128)(2,1)}, u32[]{:S(2)}) copy-start(bf16[1,256,128]{2,1,0:T(8,128)(2,1)} %param.10) | copy-start | bytes 196612
  10.3 49.2 %copy-start.3 = (bf16[1,512,1024]{2,1,0:T(8,128)(2,1)S(1)}, bf16[1,512,1024]{2,1,0:T(8,128)(2,1)}, u32[]{:S(2)}) copy-start(bf16[1,512,1024]{2,1,0:T(8,128)(2,1)} %param.12) | copy-start | bytes 3145732
  15.8 43.7 %copy-start.2 = (bf16[1,1024,512]{2,1,0:T(8,128)(2,1)S(1)}, bf16[1,1024,512]{2,1,0:T(8,128)(2,1)}, u32[]{:S(2)}) copy-start(bf16[1,1024,512]{2,1,0:T(8,128)(2,1)} %param.11) | copy-start | bytes 3145732
  88.6 10.4 %copy-start.4 = (bf16[1024,128]{1,0:T(8,128)(2,1)S(1)}, bf16[1024,128]{1,0:T(8,128)(2,1)}, u32[]{:S(2)}) copy-start(bf16[1024,128]{1,0:T(8,128)(2,1)} %keys_ref.1) | copy-start | bytes 786436
